TPU v7x, 128 devices: a whole 4x4x4 slice. The times are simulated.
128 devices in a mesh: dp: 16 (over y, z_lo, core), section: 8 (over x, z_hi).
Axes of the slice: x: 4, y: 4, z: 4 (z_hi: 2, z_lo: 2; z = z_hi * 2 + z_lo), core: 2. Of those that a mesh axis runs over, the one named last changes fastest.
Arguments:
- enc_states: bfloat16 [4096, 4096], P('dp', 'section'), may hold values from -6 to 6
- queries: bfloat16 [8, 6144, 2048], P('section', 'dp'), may hold values from -40 to 40
- cotangent: bfloat16 [8, 6144, 2048], P('section', 'dp'), may hold values from -24 to 24
- enc_lengths: int32 [16], P('dp'), may hold values from 64 to 256, as said below
- key_weight: bfloat16 [8, 4096, 2048], P('section', 'dp'), may hold values from -0.09375 to 0.09375
- value_weight: bfloat16 [8, 4096, 2048], P('section', 'dp'), may hold values from -0.09375 to 0.09375
- key_down: bfloat16 [8, 4096, 16], P('section'), may hold values from -0.09375 to 0.09375
- key_up: bfloat16 [8, 16, 2048], P('section'), may hold values from -1.5 to 1.5
- value_down: bfloat16 [8, 4096, 16], P('section'), may hold values from -0.09375 to 0.09375
- value_up: bfloat16 [8, 16, 2048], P('section'), may hold values from -1.5 to 1.5
Outputs:
- enc_grad: bfloat16 [4096, 4096], P('dp', 'section')
- key_down_grad: float32 [8, 4096, 16], P('section')
- key_up_grad: float32 [8, 16, 2048], P('section')
- value_down_grad: float32 [8, 4096, 16], P('section')
- value_up_grad: float32 [8, 16, 2048], P('section')
Inputs may be any that keep to these rules, and one draw needn't show every extreme that they name: `enc_lengths`: some sequence has 256 and some 256 // 4 unpadded tokens.
All inputs are finite; a program needn't handle non-finite values.
Results may differ from a plain program's by a relative error of at most 0.03.
The roundings to bfloat16 on the way count: a program that leaves them out, or rounds other values in their place, can miss the bound.
Values may be sent and summed in bfloat16 or wider, within the bound.
A program may use at most 192 MiB of HBM per device.

v0:
```python
import jax
import jax.numpy as jnp
from jax import lax
from jax.sharding import PartitionSpec as P

HEAD_DIM = 64


adapter_scale = 0.5
masked_score = -1e30


def project(encoded, weight, down, up):
    base = jnp.dot(encoded, weight, preferred_element_type=jnp.float32)
    low_rank = jnp.dot(encoded, down, preferred_element_type=jnp.float32).astype(jnp.bfloat16)
    summed = base + adapter_scale * jnp.dot(low_rank, up, preferred_element_type=jnp.float32)
    return (summed.astype(jnp.bfloat16), low_rank)


def adapter_back(encoded, gradient, low_rank, weight, down, up):
    up_grad = adapter_scale * jnp.dot(low_rank.T, gradient, preferred_element_type=jnp.float32)
    low_grad = (adapter_scale * jnp.dot(gradient, up.T, preferred_element_type=jnp.float32)).astype(
        jnp.bfloat16
    )
    down_grad = jnp.dot(encoded.T, low_grad, preferred_element_type=jnp.float32)
    through = jnp.dot(gradient, weight.T, preferred_element_type=jnp.float32)
    through = through + jnp.dot(low_grad, down.T, preferred_element_type=jnp.float32)
    return (through, down_grad, up_grad)


def per_device(
    enc_states,
    queries,
    cotangent,
    enc_lengths,
    key_weight,
    value_weight,
    key_down,
    key_up,
    value_down,
    value_up,
):
    encoded = lax.all_gather(enc_states, "section", axis=1, tiled=True)
    key_full, value_full = (
        lax.all_gather(key_weight, "dp", axis=1, tiled=True),
        lax.all_gather(value_weight, "dp", axis=1, tiled=True),
    )
    head_count = queries.shape[2] // HEAD_DIM
    key_rows, key_low = project(encoded, key_full[0], key_down[0], key_up[0])
    value_rows, value_low = project(encoded, value_full[0], value_down[0], value_up[0])
    query_heads = queries[0].reshape(-1, head_count, HEAD_DIM)
    key_heads = key_rows.reshape(-1, head_count, HEAD_DIM)
    value_heads = value_rows.reshape(-1, head_count, HEAD_DIM)
    grad_heads = cotangent[0].reshape(-1, head_count, HEAD_DIM)
    scores = jnp.einsum("qhd,khd->hqk", query_heads, key_heads, preferred_element_type=jnp.float32)
    visible = jnp.arange(encoded.shape[0]) < enc_lengths[0]
    scores = jnp.where(visible[None, None, :], scores, masked_score)
    peak_score = jnp.max(scores, axis=2, keepdims=True)
    expo = jnp.exp(scores - peak_score)
    probs = (expo / jnp.sum(expo, axis=2, keepdims=True)).astype(jnp.bfloat16)
    attended = jnp.einsum("hqk,khd->qhd", probs, value_heads, preferred_element_type=jnp.float32)
    row_inner = jnp.sum(attended * grad_heads.astype(jnp.float32), axis=2)
    dprobs = jnp.einsum("qhd,khd->hqk", grad_heads, value_heads, preferred_element_type=jnp.float32)
    dscores = (probs.astype(jnp.float32) * (dprobs - row_inner.T[:, :, None])).astype(jnp.bfloat16)
    dvalues = (
        jnp.einsum("hqk,qhd->khd", probs, grad_heads, preferred_element_type=jnp.float32)
        .reshape(encoded.shape[0], -1)
        .astype(jnp.bfloat16)
    )
    dkeys = (
        jnp.einsum("hqk,qhd->khd", dscores, query_heads, preferred_element_type=jnp.float32)
        .reshape(encoded.shape[0], -1)
        .astype(jnp.bfloat16)
    )
    key_through, key_down_grad, key_up_grad = adapter_back(
        encoded, dkeys, key_low, key_full[0], key_down[0], key_up[0]
    )
    value_through, value_down_grad, value_up_grad = adapter_back(
        encoded, dvalues, value_low, value_full[0], value_down[0], value_up[0]
    )
    partial_value = (key_through + value_through).astype(jnp.bfloat16).astype(jnp.float32)
    key_down_grad, key_up_grad, value_down_grad, value_up_grad = lax.psum(
        (key_down_grad, key_up_grad, value_down_grad, value_up_grad), "dp"
    )
    columns = enc_states.shape[1]
    summed = lax.psum(partial_value.astype(jnp.bfloat16), "section").astype(jnp.float32)
    offset = lax.axis_index("section") * columns
    own_share = lax.dynamic_slice_in_dim(summed, offset, columns, 1)
    return (
        own_share.astype(jnp.bfloat16),
        key_down_grad[None],
        key_up_grad[None],
        value_down_grad[None],
        value_up_grad[None],
    )


def solution(mesh):
    return jax.shard_map(
        per_device,
        mesh=mesh,
        in_specs=(
            P("dp", "section"),
            P("section", "dp", None),
            P("section", "dp", None),
            P("dp"),
            P("section", "dp", None),
            P("section", "dp", None),
            P("section", None, None),
            P("section", None, None),
            P("section", None, None),
            P("section", None, None),
        ),
        out_specs=(
            P("dp", "section"),
            P("section", None, None),
            P("section", None, None),
            P("section", None, None),
            P("section", None, None),
        ),
        check_vma=False,
    )
```

profile of v0, /device:TPU:1, one launch (start us, length us, event | category | flops | bytes accessed | tf_op | source)
XLA Modules:
  0.0 587.0 jit_solution(5575888198121661408)
XLA Ops:
  7.2 0.0 copy-start
  7.2 0.0 all-gather.4.cloned.1.call-start
  7.2 0.7 all-gather.4.cloned.1.call-update
  7.9 0.0 all-gather.6.cloned.1.call-start
  8.0 0.7 all-gather.6.cloned.1.call-update
  8.7 0.0 all-gather.8.cloned.1.call-start
  8.7 0.7 all-gather.8.cloned.1.call-update
  9.4 0.0 all-reduce.4.cloned.1.call-start
  9.5 1.6 copy.22
  11.8 1.6 copy.24
  13.4 0.5 iota_compare_fusion
  13.9 56.3 %all-gather.4.cloned.1.call-done = bf16[256,4096]{1,0:T(8,128)(2,1)} async-done(((bf16[256,512]{1,0:T(8,128)(2,1)}), bf16[256,4096]{1,0:T(8,128)(2,1)}) %all-gather.4.cloned.1.call-update) | async-done | bytes 2097168 | tf_op jit(solution)/shard_map/all_gather | solution.py:43
  70.2 0.0 copy-done
  70.2 2.4 convolution_convert_fusion.2
  72.6 2.3 convolution_convert_fusion.1
  74.8 88.7 %all-gather.6.cloned.1.call-done = bf16[1,4096,2048]{2,1,0:T(8,128)(2,1)} async-done(((bf16[1,256,2048]{2,1,0:T(8,128)(2,1)}), bf16[1,4096,2048]{2,1,0:T(8,128)(2,1)}) %all-gather.6.cloned.1.call-update) | async-done | bytes 16777232 | tf_op jit(solution)/shard_map/all_gather | solution.py:45
  163.5 8.1 %fusion.7 = f32[256,2048]{1,0:T(8,128)S(1)} fusion(bf16[256,4096]{1,0:T(8,128)(2,1)S(1)} %copy-done.2, bf16[1,4096,2048]{2,1,0:T(8,128)(2,1)} %all-gather.6.cloned.1.call-done), kind=kOutput, calls=%fused_computation.7 | convolution fusion | flops 4294967296 | bytes 20971520 | tf_op jit(solution)/shard_map/dot_general | solution.py:14
  171.7 0.5 fusion.27
  172.1 1.3 copy.21
  173.4 84.2 %all-gather.8.cloned.1.call-done = bf16[1,4096,2048]{2,1,0:T(8,128)(2,1)} async-done(((bf16[1,256,2048]{2,1,0:T(8,128)(2,1)}), bf16[1,4096,2048]{2,1,0:T(8,128)(2,1)}) %all-gather.8.cloned.1.call-update) | async-done | bytes 16777232 | tf_op jit(solution)/shard_map/all_gather | solution.py:46
  257.7 8.1 %fusion.3 = f32[256,2048]{1,0:T(8,128)S(1)} fusion(bf16[256,4096]{1,0:T(8,128)(2,1)S(1)} %copy-done.2, bf16[1,4096,2048]{2,1,0:T(8,128)(2,1)} %all-gather.8.cloned.1.call-done), kind=kOutput, calls=%fused_computation.3 | convolution fusion | flops 4294967296 | bytes 20971520 | tf_op jit(solution)/shard_map/dot_general | solution.py:14
  265.8 0.5 fusion.28
  266.3 1.3 copy.23
  267.6 11.0 %fusion.47 = (f32[32,384]{1,0:T(8,128)S(1)}, f32[32,384,256]{1,2,0:T(8,128)}) fusion(pred[256]{0:T(512)(128)(4,1)} %iota_compare_fusion, bf16[256,32,64]{0,2,1:T(8,128)(2,1)} %bitcast.121, bf16[384,32,64]{0,2,1:T(8,128)(2,1)} %bitcast.119), kind=kOutput, calls=%fused_computation.60 | convolution fusion | flops 412090624 | bytes 15253760 | tf_op jit(solution)/shard_map/sub | solution.py:59
  278.6 8.8 %divide_convert_fusion = bf16[32,384,256]{1,2,0:T(8,128)(2,1)} fusion(f32[32,384,256]{1,2,0:T(8,128)} %get-tuple-element.10, f32[32,384]{1,0:T(8,128)S(1)} %get-tuple-element.9), kind=kLoop, calls=%fused_computation.15 | loop fusion | flops 6291456 | bytes 18923520 | tf_op jit(solution)/shard_map/convert_element_type | solution.py:60
  287.4 5.1 convolution_convert_fusion
  292.5 1.7 fusion.24
  294.3 8.5 %fusion.31 = bf16[32,256,64]{1,2,0:T(8,128)(2,1)} fusion(bf16[384,32,64]{0,2,1:T(8,128)(2,1)} %bitcast.120, bf16[32,384,256]{1,2,0:T(8,128)(2,1)} %divide_convert_fusion, f32[32,384]{1,0:T(8,128)} %bitcast.122, bf16[256,32,64]{0,2,1:T(8,128)(2,1)} %bitcast.114, bf16[384,32,64]{0,2,1:T(8,128)(2,1)} %bitcast.108), kind=kOutput, calls=%fused_computation.41 | convolution fusion | flops 818413568 | bytes 11583488 | tf_op jit(solution)/shard_map/hqk,qhd->khd/dot_general | solution.py:71
  302.7 2.1 fusion.36
  304.8 0.2 fusion.37
  305.1 13.0 %fusion.5 = f32[256,4096]{1,0:T(8,128)} fusion(bf16[256,2048]{0,1:T(8,128)(2,1)} %bitcast.117, bf16[1,4096,2048]{2,1,0:T(8,128)(2,1)} %all-gather.6.cloned.1.call-done), kind=kOutput, calls=%fused_computation.5 | convolution fusion | flops 4294967296 | bytes 22020096 | tf_op jit(solution)/shard_map/dot_general | solution.py:26
  318.1 5.0 convolution_add_fusion.1
  323.0 10.1 %fusion.1 = f32[256,4096]{1,0:T(8,128)} fusion(bf16[256,2048]{0,1:T(8,128)(2,1)S(1)} %bitcast.112, bf16[1,4096,2048]{2,1,0:T(8,128)(2,1)} %all-gather.8.cloned.1.call-done), kind=kOutput, calls=%fused_computation.1 | convolution fusion | flops 4294967296 | bytes 22020096 | tf_op jit(solution)/shard_map/dot_general | solution.py:26
  333.2 5.5 fusion.21
  338.7 0.0 all-reduce.4.cloned.1.call-update
  338.8 0.0 all-reduce.6.cloned.1.call-start
  338.8 2.3 fusion.30
  341.1 1.0 fusion.29
  342.1 1.1 convolution_bitcast_fusion.1
  343.2 1.1 convolution_bitcast_fusion
  344.3 0.0 all-reduce.6.cloned.1.call-update
  344.3 104.6 %all-reduce.4.cloned.1.call-done = bf16[256,4096]{1,0:T(8,128)(2,1)} async-done(((bf16[256,4096]{1,0:T(8,128)(2,1)}), bf16[256,4096]{1,0:T(8,128)(2,1)}) %all-reduce.4.cloned.1.call-update) | async-done | bytes 2097168 | tf_op jit(solution)/shard_map/psum | solution.py:86
  449.0 1.7 convert_convert_fusion
  450.6 123.3 %all-reduce.6.cloned.1.call-done = (f32[1,4096,16]{1,2,0:T(8,128)}, f32[1,16,2048]{2,1,0:T(8,128)}, f32[1,4096,16]{1,2,0:T(8,128)}, f32[1,16,2048]{2,1,0:T(8,128)}) async-done(((f32[1,4096,16]{1,2,0:T(8,128)}, f32[1,16,2048]{2,1,0:T(8,128)}, f32[1,4096,16]{1,2,0:T(8,128)}, f32[1,16,2048]{2,1,0:T(8,128)}), (f32[1,4096,16]{1,2,0:T(8,128)}, f32[1,16,2048]{2,1,0:T(8,128)}, f32[1,4096,16]{1,2,0:T(8,128)}, ...) | async-done | bytes 786448 | tf_op jit(solution)/shard_map/psum | solution.py:82
  574.0 1.7 copy.35
  575.6 1.6 copy.36
  577.2 1.7 copy.37
  578.9 1.6 copy.38
  (20 shorter events, 0.0 us)
Async XLA Ops:
  7.2 63.0 %copy-start = (bf16[1,4096,16]{1,2,0:T(8,128)(2,1)S(1)}, bf16[1,4096,16]{1,2,0:T(8,128)(2,1)}, u32[]{:S(2)}) copy-start(bf16[1,4096,16]{1,2,0:T(8,128)(2,1)} %param.16) | copy-start | bytes 393220
  7.2 2.3 copy-start.5
  7.2 4.6 copy-start.6
  7.2 63.0 %all-gather.4.cloned.1.call-start = ((), (), s32[]{:S(2)}) async-start(), calls=%async_computation | async-start | bytes 2359296 | tf_op jit(solution)/shard_map/all_gather | solution.py:43
  7.9 155.6 %all-gather.6.cloned.1.call-start = ((), (), s32[]{:S(2)}) async-start(), calls=%async_computation.1 | async-start | bytes 17825792 | tf_op jit(solution)/shard_map/all_gather | solution.py:45
  8.7 249.0 %all-gather.8.cloned.1.call-start = ((), (), s32[]{:S(2)}) async-start(), calls=%async_computation.2 | async-start | bytes 17825792 | tf_op jit(solution)/shard_map/all_gather | solution.py:46
  9.4 439.5 %all-reduce.4.cloned.1.call-start = ((), (), s32[]{:S(2)}) async-start(), calls=%async_computation.3 | async-start | bytes 4194304 | tf_op jit(solution)/shard_map/psum | solution.py:86
  11.1 61.5 %copy-start.7 = (bf16[1,4096,16]{1,2,0:T(8,128)(2,1)S(1)}, bf16[1,4096,16]{1,2,0:T(8,128)(2,1)}, u32[]{:S(2)}) copy-start(bf16[1,4096,16]{1,2,0:T(8,128)(2,1)} %param.18) | copy-start | bytes 393220
  70.2 93.3 %copy-start.2 = (bf16[256,4096]{1,0:T(8,128)(2,1)S(1)}, bf16[256,4096]{1,0:T(8,128)(2,1)}, u32[]{:S(2)}) copy-start(bf16[256,4096]{1,0:T(8,128)(2,1)} %all-gather.4.cloned.1.call-done) | copy-start | bytes 6291460
  74.8 96.8 %copy-start.8 = (bf16[1,16,2048]{2,1,0:T(8,128)(2,1)S(1)}, bf16[1,16,2048]{2,1,0:T(8,128)(2,1)}, u32[]{:S(2)}) copy-start(bf16[1,16,2048]{2,1,0:T(8,128)(2,1)} %param.17) | copy-start | bytes 196612
  173.4 92.3 %copy-start.9 = (bf16[1,16,2048]{2,1,0:T(8,128)(2,1)S(1)}, bf16[1,16,2048]{2,1,0:T(8,128)(2,1)}, u32[]{:S(2)}) copy-start(bf16[1,16,2048]{2,1,0:T(8,128)(2,1)} %param.19) | copy-start | bytes 196612
  278.6 8.8 %copy-start.3 = (bf16[1,384,2048]{1,2,0:T(8,128)(2,1)S(1)}, bf16[1,384,2048]{1,2,0:T(8,128)(2,1)}, u32[]{:S(2)}) copy-start(bf16[1,384,2048]{1,2,0:T(8,128)(2,1)} %copy.24) | copy-start | bytes 4718596
  287.4 5.1 copy-start.1
  287.4 5.1 copy-start.4
  305.1 13.0 %copy-start.10 = (bf16[256,16]{0,1:T(8,128)(2,1)S(1)}, bf16[256,16]{0,1:T(8,128)(2,1)}, u32[]{:S(2)}) copy-start(bf16[256,16]{0,1:T(8,128)(2,1)} %fusion.36) | copy-start | bytes 24580
  338.8 235.2 %all-reduce.6.cloned.1.call-start = ((), (), s32[]{:S(2)}) async-start(), calls=%async_computation.4 | async-start | bytes 1572864 | tf_op jit(solution)/shard_map/psum | solution.py:82
Sparse Core Ops, SparseCore 0:
  10.2 59.9 all-gather.3
  71.9 91.5 all-gather.5
  165.2 92.3 all-gather.7
  338.9 110.0 all-reduce.3
  452.1 121.8 all-reduce.5
where the time goes:
time: 587 us
  waiting for transfers between devices  459 us (78%)
  matrix products  89.6 us (15%)
  between operations  14.6 us (2%)
  local copies, waits for them, and re-layouts  12.3 us (2%)
  other arithmetic  11 us (2%)
    psum x1, waiting for transfers between devices, per_device(): lax.psum((key_down_grad, key_up_grad, value_down_grad, value_up_grad), 'dp')  123 us
    psum x1, waiting for transfers between devices, per_device(): lax.psum(partial_value.astype(jnp.bfloat16), 'section').astype(jnp.float32)  105 us
    all_gather x1, waiting for transfers between devices, per_device(): lax.all_gather(key_weight, 'dp', axis=1, tiled=True)  88.7 us
    all_gather x1, waiting for transfers between devices, per_device(): lax.all_gather(value_weight, 'dp', axis=1, tiled=True)  84.2 us
    all_gather x1, waiting for transfers between devices, per_device(): encoded = lax.all_gather(enc_states, 'section', axis=1, tiled=True)  56.3 us
    dot_general x2, matrix products, adapter_back(): through = jnp.dot(gradient, weight.T, preferred_element_type=jnp.float32)  23.1 us
    dot_general x2, matrix products, project(): base = jnp.dot(encoded, weight, preferred_element_type=jnp.float32)  16.2 us
  transfers between devices with their start and end apart: 5, of which 5 were waited for; matrix products, arithmetic and copies ran while one was open for 4% of the time, Pallas kernels for 0%

commit v1 on v0

v1 whole, which is shorter than its diff:
```python
import functools

import jax
import jax.numpy as jnp
from jax import lax
from jax.experimental import pallas as pl
from jax.experimental.pallas import tpu as pltpu
from jax.sharding import PartitionSpec as P

HEAD_DIM = 64
MESH = pl.DeviceIdType.MESH
adapter_scale = 0.5
masked_score = -1e30
F32 = jnp.float32
BF16 = jnp.bfloat16

CHUNK = 256
BLOCK = 256
V_ZFIRST = 1

NT = (((1,), (1,)), ((), ()))
TN = (((0,), (0,)), ((), ()))


def dot_nt(a, b):
    return lax.dot_general(a, b, NT, preferred_element_type=F32)


def dot_tn(a, b):
    return lax.dot_general(a, b, TN, preferred_element_type=F32)


def kernel(
    chunks,
    enc_hbm, q_hbm, g_hbm, len_ref, kw_hbm, vw_hbm, kd_hbm, ku_hbm, vd_hbm, vu_hbm,
    out_ref, adapt_ref,
    W, E, Q, G, down, up, low, lowg, dkv, stage, out_recv, A, A_recv, A_all,
    local_sem, own_sem, w_send, w_recv, e_send, e_recv, o_send, o_recv, r_send, r_recv, a_send, a_recv,
):
    dp = lax.axis_index("dp")
    sec = lax.axis_index("section")
    c, zl, y = lax.rem(dp, 2), lax.rem(dp // 2, 2), dp // 4
    yp, ym, yo = lax.rem(y + 1, 4), lax.rem(y + 3, 4), lax.rem(y + 2, 4)

    def did(y_, z_, c_):
        return ((y_ * 2 + z_) * 2 + c_, sec)

    UP, DN, ZM, CM = did(yp, zl, c), did(ym, zl, c), did(y, 1 - zl, c), did(y, zl, 1 - c)

    def dp_peer(o):
        return lax.rem(dp + o, 16)

    def sec_peer(o):
        return lax.rem(sec + o, 8)

    barrier = pltpu.get_barrier_semaphore()
    for o in range(1, 16):
        pl.semaphore_signal(barrier, inc=1, device_id=(dp_peer(o), sec), device_id_type=MESH)
    for o in range(1, 8):
        pl.semaphore_signal(barrier, inc=1, device_id=(dp, sec_peer(o)), device_id_type=MESH)

    own = []
    for t, w in enumerate((kw_hbm, vw_hbm)):
        for j in range(chunks):
            own.append(
                pltpu.make_async_copy(
                    w.at[0, :, pl.ds(j * CHUNK, CHUNK)], W.at[t, j, y, zl, c], own_sem.at[t, j]
                )
            )
    columns = enc_hbm.shape[1]
    own_columns = pl.ds(pl.multiple_of(sec * columns, columns), columns)
    local = [
        pltpu.make_async_copy(enc_hbm, E.at[:, own_columns], local_sem.at[0]),
        pltpu.make_async_copy(q_hbm.at[0], Q, local_sem.at[1]),
        pltpu.make_async_copy(g_hbm.at[0], G, local_sem.at[2]),
        pltpu.make_async_copy(kd_hbm.at[0], down.at[0], local_sem.at[3]),
        pltpu.make_async_copy(vd_hbm.at[0], down.at[1], local_sem.at[4]),
        pltpu.make_async_copy(ku_hbm.at[0], up.at[0], local_sem.at[5]),
        pltpu.make_async_copy(vu_hbm.at[0], up.at[1], local_sem.at[6]),
    ]
    for copy in own + local:
        copy.start()
    for copy in own:
        copy.wait()
    pl.semaphore_wait(barrier, 22)

    def enc_copy(o):
        return pltpu.make_async_remote_copy(
            src_ref=enc_hbm, dst_ref=E.at[:, own_columns], send_sem=e_send.at[o], recv_sem=e_recv.at[o],
            device_id=(dp, sec_peer(o)), device_id_type=MESH,
        )

    def enc_arrival(o):
        src = lax.rem(sec + 8 - o, 8)
        cols = pl.ds(pl.multiple_of(src * columns, columns), columns)
        return pltpu.make_async_remote_copy(
            src_ref=enc_hbm, dst_ref=E.at[:, cols], send_sem=e_send.at[o], recv_sem=e_recv.at[o],
            device_id=(dp, src), device_id_type=MESH,
        )

    for o in range(1, 8):
        enc_copy(o).start()

    def rcopy(t, j, n, dev, ref):
        return pltpu.make_async_remote_copy(
            src_ref=ref, dst_ref=ref, send_sem=w_send.at[t, j, n], recv_sem=w_recv.at[t, j, n],
            device_id=dev, device_id_type=MESH,
        )

    def blk(t, j, y_, z_):
        return W.at[t, j, y_, z_, c]

    def pair(t, j, y_, c_):
        return W.at[t, j, y_, :, c_]

    def half(t, j, y_, h):
        return W.at[t, j, y_, zl, c, pl.ds(128 * h, 128)]

    def out(t, j, n, zf):
        if n == 0:
            return rcopy(t, j, n, ZM, blk(t, j, y, zl))
        if n in (1, 2):
            return rcopy(t, j, n, UP if n == 1 else DN, pair(t, j, y, c) if zf else blk(t, j, y, zl))
        if n == 3:
            return rcopy(t, j, n, UP, blk(t, j, ym, 0) if zf else half(t, j, ym, 0))
        if n == 4:
            return rcopy(t, j, n, DN, blk(t, j, yp, 1) if zf else half(t, j, yp, 1))
        if n <= 8:
            return rcopy(t, j, n, CM, pair(t, j, (y, ym, yp, yo)[n - 5], c))
        return rcopy(t, j, n, ZM, blk(t, j, (ym, yp, yo)[n - 9], zl))

    def inc(t, j, n, zf):
        if n == 0:
            return rcopy(t, j, n, ZM, blk(t, j, y, 1 - zl))
        if n in (1, 2):
            y_ = ym if n == 1 else yp
            return rcopy(t, j, n, DN if n == 1 else UP, pair(t, j, y_, c) if zf else blk(t, j, y_, zl))
        if n == 3:
            return rcopy(t, j, n, DN, blk(t, j, yo, 0) if zf else half(t, j, yo, 0))
        if n == 4:
            return rcopy(t, j, n, UP, blk(t, j, yo, 1) if zf else half(t, j, yo, 1))
        if n <= 8:
            return rcopy(t, j, n, CM, pair(t, j, (y, ym, yp, yo)[n - 5], 1 - c))
        return rcopy(t, j, n, ZM, blk(t, j, (ym, yp, yo)[n - 9], 1 - zl))

    def go(t, j, zf, *ns):
        for n in ns:
            out(t, j, n, zf).start()

    def wt(t, j, zf, *ns):
        for n in ns:
            inc(t, j, n, zf).wait_recv()

    def st1(t, j, zf):
        if zf:
            go(t, j, zf, 0)
        else:
            go(t, j, zf, 1, 2, 0)

    def st2(t, j, zf):
        if zf:
            wt(t, j, zf, 0)
            go(t, j, zf, 1, 2, 5)
        else:
            wt(t, j, zf, 1, 2)
            go(t, j, zf, 3, 4, 9, 10)
            wt(t, j, zf, 0)
            go(t, j, zf, 5)

    def st3(t, j, zf):
        if zf:
            wt(t, j, zf, 1, 2)
            go(t, j, zf, 3, 4, 6, 7)
        else:
            wt(t, j, zf, 3, 4)
            go(t, j, zf, 11)
            wt(t, j, zf, 9, 10)
            go(t, j, zf, 6, 7)

    def st4(t, j, zf):
        wt(t, j, zf, *((3, 4) if zf else (11,)))
        go(t, j, zf, 8)

    def st5(t, j, zf):
        wt(t, j, zf, 5, 6, 7, 8)

    def sent(t, j, zf):
        for n in range(9 if zf else 12):
            out(t, j, n, zf).wait_send()

    def routed(fn, j):
        fn(0, j, True)

        @pl.when(j >= chunks - V_ZFIRST)
        def _():
            fn(1, j, True)

        @pl.when(j < chunks - V_ZFIRST)
        def _():
            fn(1, j, False)

    def first():
        for copy in local:
            copy.wait()
        for o in range(1, 8):
            enc_arrival(o).wait_recv()
        for t in range(2):
            low[t] = jnp.dot(E[...], down[t], preferred_element_type=F32).astype(BF16)
            lowg[t] = jnp.zeros(lowg.shape[1:], F32)

    def compute(j):
        cols = pl.ds(pl.multiple_of(j * CHUNK, CHUNK), CHUNK)
        rows = []
        for t in range(2):
            weight = W[t, j].reshape(16 * BLOCK, CHUNK)
            base = jnp.dot(E[...], weight, preferred_element_type=F32)
            base = base + adapter_scale * jnp.dot(low[t], up[t, :, cols], preferred_element_type=F32)
            rows.append(base.astype(BF16))
        key_rows, value_rows = rows
        q, g = Q[:, cols], G[:, cols]
        lane = lax.broadcasted_iota(jnp.int32, (1, CHUNK), 1) // HEAD_DIM
        visible = lax.broadcasted_iota(jnp.int32, (BLOCK, 1), 0) < len_ref[0]
        dkeys = jnp.zeros((BLOCK, CHUNK), F32)
        dvalues = jnp.zeros((BLOCK, CHUNK), F32)
        zero = jnp.zeros((), BF16)
        for h in range(CHUNK // HEAD_DIM):
            here = lane == h
            scores = dot_nt(jnp.where(here, key_rows, zero), q)
            scores = jnp.where(visible, scores, masked_score)
            expo = jnp.exp(scores - jnp.max(scores, axis=0, keepdims=True))
            probs = (expo * (1.0 / jnp.sum(expo, axis=0, keepdims=True))).astype(BF16)
            dprobs = dot_nt(jnp.where(here, value_rows, zero), g)
            wide = probs.astype(F32)
            inner = jnp.sum(wide * dprobs, axis=0, keepdims=True)
            dscores = (wide * (dprobs - inner)).astype(BF16)
            dvalues = jnp.where(here, jnp.dot(probs, g, preferred_element_type=F32), dvalues)
            dkeys = jnp.where(here, jnp.dot(dscores, q, preferred_element_type=F32), dkeys)
        for t, grad in enumerate((dkeys, dvalues)):
            grad = grad.astype(BF16)
            dkv[t, j] = grad
            lowg[t] += dot_nt(grad, up[t, :, cols])
            up_grad = adapter_scale * dot_tn(low[t], grad)
            for half_ in range(2):
                A[2 * j + half_, pl.ds(16 * t, 16), 256:384] = up_grad[:, 128 * half_ : 128 * half_ + 128]

    def slot(k, carry):
        for i, fn in enumerate((st1, st2, st3, st4, st5)):
            j = k - i

            @pl.when(jnp.logical_and(j >= 0, j < chunks))
            def _(fn=fn, j=j):
                routed(fn, j)

        @pl.when(k == 4)
        def _():
            first()

        @pl.when(k >= 4)
        def _():
            compute(k - 4)

        return carry

    lax.fori_loop(0, chunks + 4, slot, 0)

    for t in range(2):
        low[t] = (adapter_scale * lowg[t]).astype(BF16)

    def down_grad(r, carry):
        e = E[:, pl.ds(pl.multiple_of(r * BLOCK, BLOCK), BLOCK)]
        for t in range(2):
            A[r, pl.ds(16 * t, 16), 0:256] = dot_tn(low[t], e)
        return carry

    lax.fori_loop(0, 16, down_grad, 0)

    def reduce_copy(o):
        return pltpu.make_async_remote_copy(
            src_ref=A.at[dp_peer(o)], dst_ref=A_recv.at[o], send_sem=r_send.at[o], recv_sem=r_recv.at[o],
            device_id=(dp_peer(o), sec), device_id_type=MESH,
        )

    for o in range(1, 16):
        reduce_copy(o).start()

    def partial_copy(o):
        return pltpu.make_async_remote_copy(
            src_ref=stage.at[o], dst_ref=out_recv.at[o], send_sem=o_send.at[o], recv_sem=o_recv.at[o],
            device_id=(dp, sec_peer(o)), device_id_type=MESH,
        )

    def back(i, carry):
        o = i + 1
        p = lax.rem(sec + o, 8)
        for b in range(2):
            r = 2 * p + b
            r_y, r_z, r_c = r // 4, lax.rem(r // 2, 2), lax.rem(r, 2)
            acc = jnp.zeros((BLOCK, BLOCK), F32)
            for t in range(2):
                wide = jnp.concatenate([W[t, j, r_y, r_z, r_c] for j in range(chunks)], axis=1)
                grad = jnp.concatenate([dkv[t, j] for j in range(chunks)], axis=1)
                acc = acc + dot_nt(grad, wide)
                d = down[t, pl.ds(pl.multiple_of(r * BLOCK, BLOCK), BLOCK), :]
                acc = acc + dot_nt(low[t], d)
            stage[lax.rem(o, 8), :, b * BLOCK : (b + 1) * BLOCK] = acc.astype(BF16)

        @pl.when(o < 8)
        def _():
            partial_copy(o).start()

        return carry

    lax.fori_loop(0, 8, back, 0)

    total = A[dp]
    for o in range(1, 16):
        reduce_copy(o).wait_recv()
        total = total + A_recv[o]
    A_all[dp] = total

    def spread_copy(o, index):
        return pltpu.make_async_remote_copy(
            src_ref=A_all.at[index], dst_ref=A_all.at[index], send_sem=a_send.at[o], recv_sem=a_recv.at[o],
            device_id=(dp_peer(o), sec), device_id_type=MESH,
        )

    for o in range(1, 16):
        spread_copy(o, dp).start()

    summed = stage[0].astype(F32)
    for o in range(1, 8):
        partial_copy(o).wait_recv()
        summed = summed + out_recv[o].astype(F32)
    out_ref[...] = summed.astype(BF16)

    for o in range(1, 16):
        spread_copy(o, lax.rem(dp + 16 - o, 16)).wait_recv()
    adapt_ref[...] = A_all[...]

    def drain(j, carry):
        routed(sent, j)
        return carry

    lax.fori_loop(0, chunks, drain, 0)
    for o in range(1, 8):
        enc_copy(o).wait_send()
        partial_copy(o).wait_send()
    for o in range(1, 16):
        reduce_copy(o).wait_send()
        spread_copy(o, dp).wait_send()


def per_device(
    enc_states, queries, cotangent, enc_lengths, key_weight, value_weight, key_down, key_up, value_down, value_up
):
    inner = queries.shape[2]
    chunks = inner // CHUNK
    width = key_down.shape[1]
    columns = enc_states.shape[1]
    hbm = pl.BlockSpec(memory_space=pl.ANY)
    vmem = pl.BlockSpec(memory_space=pltpu.VMEM)
    dma = pltpu.SemaphoreType.DMA
    out, adapt = pl.pallas_call(
        functools.partial(kernel, chunks),
        out_shape=(
            jax.ShapeDtypeStruct((BLOCK, columns), BF16),
            jax.ShapeDtypeStruct((16, 32, 384), F32),
        ),
        in_specs=[hbm, hbm, hbm, pl.BlockSpec(memory_space=pltpu.SMEM)] + [hbm] * 6,
        out_specs=(vmem, vmem),
        scratch_shapes=[
            pltpu.VMEM((2, chunks, 4, 2, 2, BLOCK, CHUNK), BF16),
            pltpu.VMEM((BLOCK, width), BF16),
            pltpu.VMEM(queries.shape[1:], BF16),
            pltpu.VMEM(cotangent.shape[1:], BF16),
            pltpu.VMEM((2, width, 16), BF16),
            pltpu.VMEM((2, 16, inner), BF16),
            pltpu.VMEM((2, BLOCK, 16), BF16),
            pltpu.VMEM((2, BLOCK, 16), F32),
            pltpu.VMEM((2, chunks, BLOCK, CHUNK), BF16),
            pltpu.VMEM((8, BLOCK, columns), BF16),
            pltpu.VMEM((8, BLOCK, columns), BF16),
            pltpu.VMEM((16, 32, 384), F32),
            pltpu.VMEM((16, 32, 384), F32),
            pltpu.VMEM((16, 32, 384), F32),
            dma((7,)),
            dma((2, chunks)),
            dma((2, chunks, 12)),
            dma((2, chunks, 12)),
            dma((8,)),
            dma((8,)),
            dma((8,)),
            dma((8,)),
            dma((16,)),
            dma((16,)),
            dma((16,)),
            dma((16,)),
        ],
        compiler_params=pltpu.CompilerParams(
            collective_id=0, has_side_effects=True, vmem_limit_bytes=60 * 1024 * 1024
        ),
        name="adapter_backward",
    )(
        enc_states, queries, cotangent, enc_lengths, key_weight, value_weight, key_down, key_up, value_down, value_up
    )
    down_grads = jnp.transpose(adapt[:, :, :256].reshape(16, 2, 16, 256), (1, 0, 3, 2)).reshape(2, 1, width, 16)
    up_grads = jnp.transpose(adapt[:, :, 256:].reshape(16, 2, 16, 128), (1, 2, 0, 3)).reshape(2, 1, 16, inner)
    return out, down_grads[0], up_grads[0], down_grads[1], up_grads[1]


def solution(mesh):
    return jax.shard_map(
        per_device,
        mesh=mesh,
        in_specs=(
            P("dp", "section"),
            P("section", "dp", None),
            P("section", "dp", None),
            P("dp"),
            P("section", "dp", None),
            P("section", "dp", None),
            P("section", None, None),
            P("section", None, None),
            P("section", None, None),
            P("section", None, None),
        ),
        out_specs=(
            P("dp", "section"),
            P("section", None, None),
            P("section", None, None),
            P("section", None, None),
            P("section", None, None),
        ),
        check_vma=False,
    )
```

time: 587 us -> 213 us (0.36)
  waiting for transfers between devices: 459 us -> 0 us
  Pallas kernels: 0 us -> 200 us
  matrix products: 89.6 us -> 0 us
  between operations: 14.6 us -> 1.32 us
  other arithmetic: 11 us -> 0 us
    all_gather x3 -> x0, waiting for transfers between devices: 229 us -> none  [the longest x1 88.7 us: per_device(): lax.all_gather(key_weight, 'dp', axis=1, tiled=True)]
    psum x2 -> x0, waiting for transfers between devices: 228 us -> none  [the longest x1 123 us: per_device(): lax.psum((key_down_grad, key_up_grad, value_down_grad, value_up_grad), 'dp')]
    pallas_call x0 -> x1, Pallas kernels: none -> 200 us  [per_device(): pl.pallas_call(functools.partial(kernel, chunks), out_shape=(jax.ShapeDty...]
    dot_general x19 -> x0, matrix products: 78.5 us -> none  [the longest x2 23.1 us: adapter_back(): through = jnp.dot(gradient, weight.T, preferred_element_type=jnp.float32)]
    sub x1 -> x0, matrix products: 11 us -> none  [per_device(): expo = jnp.exp(scores - peak_score)]
    convert_element_type x2 -> x0, other arithmetic: 10.5 us -> none  [the longest x1 8.83 us: per_device(): probs = (expo / jnp.sum(expo, axis=2, keepdims=True)).astype(jnp.bfloat16)]
  transfers between devices with their start and end apart: 5 -> 0, of which waited for: 5 -> 0; matrix products, arithmetic and copies ran while one was open for 4% -> 0% of each run, Pallas kernels for 0% -> 0%
where the time goes in v1:
time: 213 us; the launch traced here: 210 us
  Pallas kernels  200 us (94%)
  local copies, waits for them, and re-layouts  9.44 us (4%)
    pallas_call x1, Pallas kernels, per_device(): pl.pallas_call(functools.partial(kernel, chunks), out_shape=(jax.ShapeDty...  200 us
    unnamed x7, local copies, waits for them, and re-layouts  5.23 us

profile of v1, /device:TPU:1, one launch (start us, length us, event | category | flops | bytes accessed | tf_op | source)
XLA Modules:
  0.0 210.3 jit_solution(12020360639610335061)
XLA Ops:
  1.3 2.2 %copy.15.kd_hbm = bf16[1,4096,16]{2,1,0:T(8,128)(2,1)} copy(bf16[1,4096,16]{1,2,0:T(8,128)(2,1)} %param.16) | data formatting | bytes 262144 | tf_op args[6]
  3.5 2.3 %copy.16.vd_hbm = bf16[1,4096,16]{2,1,0:T(8,128)(2,1)} copy(bf16[1,4096,16]{1,2,0:T(8,128)(2,1)} %param.18) | data formatting | bytes 262144 | tf_op args[8]
  5.8 199.6 %adapter_backward.1 = (bf16[256,512]{1,0:T(8,128)(2,1)}, f32[16,32,384]{2,1,0:T(8,128)}) custom-call(bf16[256,512]{1,0:T(8,128)(2,1)} %enc_hbm.1, bf16[1,384,2048]{2,1,0:T(8,128)(2,1)} %q_hbm.1, bf16[1,384,2048]{2,1,0:T(8,128)(2,1)} %g_hbm.1, s32[1]{0:T(128)S(6)} %copy.28.len_ref, bf16[1,256,2048]{2,1,0:T(8,128)(2,1)} %kw_hbm.1, ...), custom_call_target="tpu_custom_call" | custom-call | tf_op jit(solution)/shard_map/adapter_backward/pallas_call | solution.py:363
  205.3 1.0 slice.24
  206.3 1.1 slice.22
  207.4 0.0 copy-start
  207.4 0.7 copy_bitcast_fusion
  208.2 0.7 copy.23
  208.9 0.7 copy.21
  209.6 0.0 copy-done
  209.6 0.7 copy.29
  (2 shorter events, 0.1 us)
Async XLA Ops:
  207.4 2.2 %copy-start = (bf16[256,512]{1,0:T(8,128)(2,1)S(1)}, bf16[256,512]{1,0:T(8,128)(2,1)}, u32[]{:S(2)}) copy-start(bf16[256,512]{1,0:T(8,128)(2,1)} %get-tuple-element.20) | copy-start | bytes 786436

commit v2 on v1

--- a/solution.py
+++ b/solution.py
@@ -33,8 +33,8 @@
 def kernel(
     chunks,
     enc_hbm, q_hbm, g_hbm, len_ref, kw_hbm, vw_hbm, kd_hbm, ku_hbm, vd_hbm, vu_hbm,
-    out_ref, adapt_ref,
-    W, E, Q, G, down, up, low, lowg, dkv, stage, out_recv, A, A_recv, A_all,
+    out_ref, kd_ref, ku_ref, vd_ref, vu_ref,
+    W, E, Q, G, down, up, low, lowg, dkv, stage, out_recv, cross, cross_recv, A, A_recv, A_all,
     local_sem, own_sem, w_send, w_recv, e_send, e_recv, o_send, o_recv, r_send, r_recv, a_send, a_recv,
 ):
     dp = lax.axis_index("dp")
@@ -50,14 +50,16 @@
     def dp_peer(o):
         return lax.rem(dp + o, 16)
 
-    def sec_peer(o):
-        return lax.rem(sec + o, 8)
+    x, zh = sec // 2, lax.rem(sec, 2)
+
+    def sec_at(dx, other):
+        return lax.rem(x + dx, 4) * 2 + (1 - zh if other else zh)
 
     barrier = pltpu.get_barrier_semaphore()
     for o in range(1, 16):
         pl.semaphore_signal(barrier, inc=1, device_id=(dp_peer(o), sec), device_id_type=MESH)
-    for o in range(1, 8):
-        pl.semaphore_signal(barrier, inc=1, device_id=(dp, sec_peer(o)), device_id_type=MESH)
+    for to in (sec_at(0, True), sec_at(1, False), sec_at(2, False), sec_at(3, False)):
+        pl.semaphore_signal(barrier, inc=1, device_id=(dp, to), device_id_type=MESH)
 
     own = []
     for t, w in enumerate((kw_hbm, vw_hbm)):
@@ -68,38 +70,46 @@
                 )
             )
     columns = enc_hbm.shape[1]
-    own_columns = pl.ds(pl.multiple_of(sec * columns, columns), columns)
+
+    def section_columns(p):
+        return pl.ds(pl.multiple_of(p * columns, columns), columns)
+
     local = [
-        pltpu.make_async_copy(enc_hbm, E.at[:, own_columns], local_sem.at[0]),
+        pltpu.make_async_copy(enc_hbm, E.at[:, section_columns(sec)], local_sem.at[0]),
         pltpu.make_async_copy(q_hbm.at[0], Q, local_sem.at[1]),
         pltpu.make_async_copy(g_hbm.at[0], G, local_sem.at[2]),
-        pltpu.make_async_copy(kd_hbm.at[0], down.at[0], local_sem.at[3]),
-        pltpu.make_async_copy(vd_hbm.at[0], down.at[1], local_sem.at[4]),
+        pltpu.make_async_copy(kd_hbm, down.at[0], local_sem.at[3]),
+        pltpu.make_async_copy(vd_hbm, down.at[1], local_sem.at[4]),
         pltpu.make_async_copy(ku_hbm.at[0], up.at[0], local_sem.at[5]),
         pltpu.make_async_copy(vu_hbm.at[0], up.at[1], local_sem.at[6]),
     ]
     for copy in own + local:
         copy.start()
-    for copy in own:
-        copy.wait()
-    pl.semaphore_wait(barrier, 22)
-
-    def enc_copy(o):
-        return pltpu.make_async_remote_copy(
-            src_ref=enc_hbm, dst_ref=E.at[:, own_columns], send_sem=e_send.at[o], recv_sem=e_recv.at[o],
-            device_id=(dp, sec_peer(o)), device_id_type=MESH,
-        )
-
-    def enc_arrival(o):
-        src = lax.rem(sec + 8 - o, 8)
-        cols = pl.ds(pl.multiple_of(src * columns, columns), columns)
-        return pltpu.make_async_remote_copy(
-            src_ref=enc_hbm, dst_ref=E.at[:, cols], send_sem=e_send.at[o], recv_sem=e_recv.at[o],
-            device_id=(dp, src), device_id_type=MESH,
-        )
-
-    for o in range(1, 8):
-        enc_copy(o).start()
+    pl.semaphore_wait(barrier, 19)
+
+    def enc_copy(n, src_ref, piece, to):
+        return pltpu.make_async_remote_copy(
+            src_ref=src_ref, dst_ref=E.at[:, section_columns(piece)], send_sem=e_send.at[n], recv_sem=e_recv.at[n],
+            device_id=(dp, to), device_id_type=MESH,
+        )
+
+    def enc_out(n):
+        if n == 0:
+            return enc_copy(n, enc_hbm, sec, sec_at(0, True))
+        if n < 4:
+            return enc_copy(n, enc_hbm, sec, sec_at(n, False))
+        mate = sec_at(0, True)
+        return enc_copy(n, E.at[:, section_columns(mate)], mate, sec_at(n - 3, False))
+
+    def enc_in(n):
+        if n == 0:
+            piece = sec_at(0, True)
+        else:
+            piece = sec_at(4 - n, False) if n < 4 else sec_at(7 - n, True)
+        return enc_copy(n, E.at[:, section_columns(piece)], piece, sec_at(0, True))
+
+    for n in range(4):
+        enc_out(n).start()
 
     def rcopy(t, j, n, dev, ref):
         return pltpu.make_async_remote_copy(
@@ -116,11 +126,25 @@
     def half(t, j, y_, h):
         return W.at[t, j, y_, zl, c, pl.ds(128 * h, 128)]
 
+    def from_hbm(t, j, n, dev):
+        w = (kw_hbm, vw_hbm)[t]
+        return pltpu.make_async_remote_copy(
+            src_ref=w.at[0, :, pl.ds(pl.multiple_of(j * CHUNK, CHUNK), CHUNK)], dst_ref=blk(t, j, y, zl),
+            send_sem=w_send.at[t, j, n], recv_sem=w_recv.at[t, j, n], device_id=dev, device_id_type=MESH,
+        )
+
+    def own_copy(t, j):
+        w = (kw_hbm, vw_hbm)[t]
+        return pltpu.make_async_copy(
+            w.at[0, :, pl.ds(pl.multiple_of(j * CHUNK, CHUNK), CHUNK)], blk(t, j, y, zl), own_sem.at[t, j]
+        )
+
     def out(t, j, n, zf):
         if n == 0:
-            return rcopy(t, j, n, ZM, blk(t, j, y, zl))
+            return from_hbm(t, j, n, ZM)
         if n in (1, 2):
-            return rcopy(t, j, n, UP if n == 1 else DN, pair(t, j, y, c) if zf else blk(t, j, y, zl))
+            dev = UP if n == 1 else DN
+            return rcopy(t, j, n, dev, pair(t, j, y, c)) if zf else from_hbm(t, j, n, dev)
         if n == 3:
             return rcopy(t, j, n, UP, blk(t, j, ym, 0) if zf else half(t, j, ym, 0))
         if n == 4:
@@ -158,6 +182,7 @@
             go(t, j, zf, 1, 2, 0)
 
     def st2(t, j, zf):
+        own_copy(t, j).wait()
         if zf:
             wt(t, j, zf, 0)
             go(t, j, zf, 1, 2, 5)
@@ -191,21 +216,21 @@
     def routed(fn, j):
         fn(0, j, True)
 
-        @pl.when(j >= chunks - V_ZFIRST)
+        @pl.when(j == V_ZFIRST)
         def _():
             fn(1, j, True)
 
-        @pl.when(j < chunks - V_ZFIRST)
+        @pl.when(j != V_ZFIRST)
         def _():
             fn(1, j, False)
 
     def first():
         for copy in local:
             copy.wait()
-        for o in range(1, 8):
-            enc_arrival(o).wait_recv()
+        for n in range(1, 7):
+            enc_in(n).wait_recv()
         for t in range(2):
-            low[t] = jnp.dot(E[...], down[t], preferred_element_type=F32).astype(BF16)
+            low[t] = dot_nt(E[...], down[t]).astype(BF16)
             lowg[t] = jnp.zeros(lowg.shape[1:], F32)
 
     def compute(j):
@@ -241,7 +266,7 @@
             lowg[t] += dot_nt(grad, up[t, :, cols])
             up_grad = adapter_scale * dot_tn(low[t], grad)
             for half_ in range(2):
-                A[2 * j + half_, pl.ds(16 * t, 16), 256:384] = up_grad[:, 128 * half_ : 128 * half_ + 128]
+                A[2 * j + half_, pl.ds(16 * t, 16), 256:384] = up_grad[:, 128 * half_ : 128 * half_ + 128].astype(BF16)
 
     def slot(k, carry):
         for i, fn in enumerate((st1, st2, st3, st4, st5)):
@@ -251,6 +276,12 @@
             def _(fn=fn, j=j):
                 routed(fn, j)
 
+        @pl.when(k == 0)
+        def _():
+            enc_in(0).wait_recv()
+            for n in range(4, 7):
+                enc_out(n).start()
+
         @pl.when(k == 4)
         def _():
             first()
@@ -269,7 +300,7 @@
     def down_grad(r, carry):
         e = E[:, pl.ds(pl.multiple_of(r * BLOCK, BLOCK), BLOCK)]
         for t in range(2):
-            A[r, pl.ds(16 * t, 16), 0:256] = dot_tn(low[t], e)
+            A[r, pl.ds(16 * t, 16), 0:256] = dot_tn(low[t], e).astype(BF16)
         return carry
 
     lax.fori_loop(0, 16, down_grad, 0)
@@ -283,15 +314,21 @@
     for o in range(1, 16):
         reduce_copy(o).start()
 
-    def partial_copy(o):
-        return pltpu.make_async_remote_copy(
-            src_ref=stage.at[o], dst_ref=out_recv.at[o], send_sem=o_send.at[o], recv_sem=o_recv.at[o],
-            device_id=(dp, sec_peer(o)), device_id_type=MESH,
+    def partial_copy(i):
+        return pltpu.make_async_remote_copy(
+            src_ref=stage.at[i], dst_ref=out_recv.at[i], send_sem=o_send.at[i], recv_sem=o_recv.at[i],
+            device_id=(dp, sec_at(i % 4 + 1, False)), device_id_type=MESH,
+        )
+
+    def cross_copy():
+        return pltpu.make_async_remote_copy(
+            src_ref=cross, dst_ref=cross_recv, send_sem=o_send.at[3], recv_sem=o_recv.at[3],
+            device_id=(dp, sec_at(0, True)), device_id_type=MESH,
         )
 
     def back(i, carry):
-        o = i + 1
-        p = lax.rem(sec + o, 8)
+        other = i < 4
+        p = lax.rem(x + lax.rem(i, 4) + 1, 4) * 2 + jnp.where(other, 1 - zh, zh)
         for b in range(2):
             r = 2 * p + b
             r_y, r_z, r_c = r // 4, lax.rem(r // 2, 2), lax.rem(r, 2)
@@ -300,22 +337,24 @@
                 wide = jnp.concatenate([W[t, j, r_y, r_z, r_c] for j in range(chunks)], axis=1)
                 grad = jnp.concatenate([dkv[t, j] for j in range(chunks)], axis=1)
                 acc = acc + dot_nt(grad, wide)
-                d = down[t, pl.ds(pl.multiple_of(r * BLOCK, BLOCK), BLOCK), :]
-                acc = acc + dot_nt(low[t], d)
-            stage[lax.rem(o, 8), :, b * BLOCK : (b + 1) * BLOCK] = acc.astype(BF16)
-
-        @pl.when(o < 8)
-        def _():
-            partial_copy(o).start()
+                d = down[t, :, pl.ds(pl.multiple_of(r * BLOCK, BLOCK), BLOCK)]
+                acc = acc + jnp.dot(low[t], d, preferred_element_type=F32)
+            stage[i, :, b * BLOCK : (b + 1) * BLOCK] = acc.astype(BF16)
+
+        for n in (0, 1, 2, 4, 5, 6):
+
+            @pl.when(i == n)
+            def _(n=n):
+                partial_copy(n).start()
 
         return carry
 
     lax.fori_loop(0, 8, back, 0)
 
-    total = A[dp]
+    total = A[dp].astype(F32)
     for o in range(1, 16):
         reduce_copy(o).wait_recv()
-        total = total + A_recv[o]
+        total = total + A_recv[o].astype(F32)
     A_all[dp] = total
 
     def spread_copy(o, index):
@@ -327,27 +366,51 @@
     for o in range(1, 16):
         spread_copy(o, dp).start()
 
-    summed = stage[0].astype(F32)
-    for o in range(1, 8):
-        partial_copy(o).wait_recv()
-        summed = summed + out_recv[o].astype(F32)
-    out_ref[...] = summed.astype(BF16)
+    def summed(first_, own_):
+        total_ = stage[own_].astype(F32)
+        for n in range(first_, first_ + 3):
+            partial_copy(n).wait_recv()
+            total_ = total_ + out_recv[n].astype(F32)
+        return total_
+
+    cross[...] = summed(0, 3).astype(BF16)
+    cross_copy().start()
 
     for o in range(1, 16):
-        spread_copy(o, lax.rem(dp + 16 - o, 16)).wait_recv()
-    adapt_ref[...] = A_all[...]
+        r = lax.rem(dp + 16 - o, 16)
+        spread_copy(o, r).wait_recv()
+    for r in range(16):
+        kd_ref[:, r * 256 : r * 256 + 256] = A_all[r, 0:16, 0:256]
+        vd_ref[:, r * 256 : r * 256 + 256] = A_all[r, 16:32, 0:256]
+        ku_ref[:, r * 128 : r * 128 + 128] = A_all[r, 0:16, 256:384]
+        vu_ref[:, r * 128 : r * 128 + 128] = A_all[r, 16:32, 256:384]
+
+    whole = summed(4, 7)
+    cross_copy().wait_recv()
+    out_ref[...] = (whole + cross_recv[...].astype(F32)).astype(BF16)
 
     def drain(j, carry):
         routed(sent, j)
         return carry
 
     lax.fori_loop(0, chunks, drain, 0)
-    for o in range(1, 8):
-        enc_copy(o).wait_send()
-        partial_copy(o).wait_send()
+    for n in range(7):
+        enc_out(n).wait_send()
+    for n in (0, 1, 2, 4, 5, 6):
+        partial_copy(n).wait_send()
+    cross_copy().wait_send()
     for o in range(1, 16):
         reduce_copy(o).wait_send()
         spread_copy(o, dp).wait_send()
+
+
+def settle(*refs):
+    sem = refs[-1]
+    copies = [pltpu.make_async_copy(refs[i], refs[5 + i], sem.at[i]) for i in range(5)]
+    for copy in copies:
+        copy.start()
+    for copy in copies:
+        copy.wait()
 
 
 def per_device(
@@ -360,28 +423,33 @@
     hbm = pl.BlockSpec(memory_space=pl.ANY)
     vmem = pl.BlockSpec(memory_space=pltpu.VMEM)
     dma = pltpu.SemaphoreType.DMA
-    out, adapt = pl.pallas_call(
+    results = pl.pallas_call(
         functools.partial(kernel, chunks),
         out_shape=(
             jax.ShapeDtypeStruct((BLOCK, columns), BF16),
-            jax.ShapeDtypeStruct((16, 32, 384), F32),
+            jax.ShapeDtypeStruct((16, width), F32),
+            jax.ShapeDtypeStruct((16, inner), F32),
+            jax.ShapeDtypeStruct((16, width), F32),
+            jax.ShapeDtypeStruct((16, inner), F32),
         ),
         in_specs=[hbm, hbm, hbm, pl.BlockSpec(memory_space=pltpu.SMEM)] + [hbm] * 6,
-        out_specs=(vmem, vmem),
+        out_specs=(vmem,) * 5,
         scratch_shapes=[
             pltpu.VMEM((2, chunks, 4, 2, 2, BLOCK, CHUNK), BF16),
             pltpu.VMEM((BLOCK, width), BF16),
             pltpu.VMEM(queries.shape[1:], BF16),
             pltpu.VMEM(cotangent.shape[1:], BF16),
-            pltpu.VMEM((2, width, 16), BF16),
+            pltpu.VMEM((2, 16, width), BF16),
             pltpu.VMEM((2, 16, inner), BF16),
             pltpu.VMEM((2, BLOCK, 16), BF16),
             pltpu.VMEM((2, BLOCK, 16), F32),
             pltpu.VMEM((2, chunks, BLOCK, CHUNK), BF16),
             pltpu.VMEM((8, BLOCK, columns), BF16),
             pltpu.VMEM((8, BLOCK, columns), BF16),
-            pltpu.VMEM((16, 32, 384), F32),
-            pltpu.VMEM((16, 32, 384), F32),
+            pltpu.VMEM((BLOCK, columns), BF16),
+            pltpu.VMEM((BLOCK, columns), BF16),
+            pltpu.VMEM((16, 32, 384), BF16),
+            pltpu.VMEM((16, 32, 384), BF16),
             pltpu.VMEM((16, 32, 384), F32),
             dma((7,)),
             dma((2, chunks)),
@@ -401,11 +469,18 @@
         ),
         name="adapter_backward",
     )(
-        enc_states, queries, cotangent, enc_lengths, key_weight, value_weight, key_down, key_up, value_down, value_up
+        enc_states, queries, cotangent, enc_lengths, key_weight, value_weight,
+        key_down[0].T, key_up, value_down[0].T, value_up,
     )
-    down_grads = jnp.transpose(adapt[:, :, :256].reshape(16, 2, 16, 256), (1, 0, 3, 2)).reshape(2, 1, width, 16)
-    up_grads = jnp.transpose(adapt[:, :, 256:].reshape(16, 2, 16, 128), (1, 2, 0, 3)).reshape(2, 1, 16, inner)
-    return out, down_grads[0], up_grads[0], down_grads[1], up_grads[1]
+    out, kd_grad, ku_grad, vd_grad, vu_grad = pl.pallas_call(
+        settle,
+        out_shape=tuple(jax.ShapeDtypeStruct(r.shape, r.dtype) for r in results),
+        in_specs=[vmem] * 5,
+        out_specs=(hbm,) * 5,
+        scratch_shapes=[dma((5,))],
+        name="results",
+    )(*results)
+    return out, kd_grad.T[None], ku_grad[None], vd_grad.T[None], vu_grad[None]
 
 
 def solution(mesh):

time: 213 us -> 170 us (0.80); the launches traced: 210 us -> 170 us
  Pallas kernels: 200 us -> 169 us
  local copies, waits for them, and re-layouts: 9.44 us -> 0 us
    pallas_call x1, Pallas kernels: 200 us -> 167 us  [per_device(): pl.pallas_call(functools.partial(kernel, chunks), out_shape=(jax.ShapeDty...]
    unnamed x7 -> x0, local copies, waits for them, and re-layouts: 5.23 us -> none
    pallas_call x0 -> x1, Pallas kernels: none -> 2.18 us  [per_device(): pl.pallas_call(settle, out_shape=tuple((jax.ShapeDtypeStruct(r.shape, r.d...]
    squeeze x3 -> x0, local copies, waits for them, and re-layouts: 2.16 us -> none  [per_device(): return (out, down_grads[0], up_grads[0], down_grads[1], up_grads[1])]
where the time goes in v2:
time: 170 us
  Pallas kernels  169 us (99%)
    pallas_call x1, Pallas kernels, per_device(): pl.pallas_call(functools.partial(kernel, chunks), out_shape=(jax.ShapeDty...  167 us

profile of v2, /device:TPU:1, one launch (start us, length us, event | category | flops | bytes accessed | tf_op | source)
XLA Modules:
  0.0 170.1 jit_solution(8393855464567973709)
XLA Ops:
  1.3 166.7 %adapter_backward.1 = (bf16[256,512]{1,0:T(8,128)(2,1)}, f32[16,4096]{1,0:T(8,128)}, f32[16,2048]{1,0:T(8,128)}, f32[16,4096]{1,0:T(8,128)}, f32[16,2048]{1,0:T(8,128)}) custom-call(bf16[256,512]{1,0:T(8,128)(2,1)} %enc_hbm.1, bf16[1,384,2048]{2,1,0:T(8,128)(2,1)} %q_hbm.1, bf16[1,384,2048]{2,1,0:T(8,128)(2,1)} %g_hbm.1, s32[1]{0:T(128)S(6)} %copy.15.len_ref, ...), custom_call_target="tpu_custom_call" | custom-call | tf_op jit(solution)/shard_map/adapter_backward/pallas_call | solution.py:426
  168.0 2.2 %results.1 = (bf16[256,512]{1,0:T(8,128)(2,1)}, f32[16,4096]{1,0:T(8,128)}, f32[16,2048]{1,0:T(8,128)}, f32[16,4096]{1,0:T(8,128)}, f32[16,2048]{1,0:T(8,128)}) custom-call(bf16[256,512]{1,0:T(8,128)(2,1)} %get-tuple-element.15.refs_0_, f32[16,4096]{1,0:T(8,128)} %get-tuple-element.16.refs_1_, f32[16,2048]{1,0:T(8,128)} %get-tuple-element.17.refs_2_, ...), custom_call_target="tpu_custom_call" | custom-call | tf_op jit(solution)/shard_map/results/pallas_call | solution.py:475

commit v3 on v0

v3 whole, which is shorter than its diff:
```python
import functools

import jax
import jax.numpy as jnp
from jax import lax
from jax.experimental import pallas as pl
from jax.experimental.pallas import tpu as pltpu
from jax.sharding import PartitionSpec as P

HEAD_DIM = 64
MESH = pl.DeviceIdType.MESH
adapter_scale = 0.5
masked_score = -1e30
F32 = jnp.float32
BF16 = jnp.bfloat16

FEATURES = 128
PACK = 2 * FEATURES
BLOCK = 256

NT = (((1,), (1,)), ((), ()))


def dot(a, b):
    return jnp.dot(a, b, preferred_element_type=F32)


def dot_nt(a, b):
    return lax.dot_general(a, b, NT, preferred_element_type=F32)


def kernel(
    chunks,
    enc_hbm, q_hbm, g_hbm, len_ref, kw_hbm, vw_hbm, kd_hbm, ku_hbm, vd_hbm, vu_hbm,
    out_ref, kd_ref, ku_ref, vd_ref, vu_ref,
    W, E, QG, lens, down, up, up_pack, low, low_t, lowg, dkv,
    stage, x_part, z_first, z_first_sum, z_sum, z_part, x_far,
    A, A_recv, A_all,
    local_sem, own_sem, q_own_sem, w_send, w_recv, q_send, q_recv,
    ez_send, ez_recv, ex_send, ex_recv, ef_send, ef_recv, len_send, len_recv,
    zf_send, zf_recv, xp_send, xp_recv, zp_send, zp_recv, far_send, far_recv,
    r_send, r_recv, a_send, a_recv,
):
    dp = lax.axis_index("dp")
    sec = lax.axis_index("section")
    c, zl, y = lax.rem(dp, 2), lax.rem(dp // 2, 2), dp // 4
    x, zh = sec // 2, lax.rem(sec, 2)
    yp, ym, yo = lax.rem(y + 1, 4), lax.rem(y + 3, 4), lax.rem(y + 2, 4)
    half = chunks * FEATURES
    columns = enc_hbm.shape[1]

    def did(y_, z_, c_):
        return ((y_ * 2 + z_) * 2 + c_, sec)

    UP, DN, ZM, CM = did(yp, zl, c), did(ym, zl, c), did(y, 1 - zl, c), did(y, zl, 1 - c)

    def dp_peer(o):
        return lax.rem(dp + o, 16)

    def sec_of(dx, zh_):
        return lax.rem(x + dx, 4) * 2 + zh_

    def x_peer(dx):
        return (dp, sec_of(dx, zh))

    z_coords = ((1 - zl, zh), (zl, 1 - zh), (1 - zl, 1 - zh))

    def z_peer(a):
        z_, h_ = z_coords[a]
        return ((y * 2 + z_) * 2 + c, x * 2 + h_)

    def remote(src, dst, send, recv, dev):
        return pltpu.make_async_remote_copy(
            src_ref=src, dst_ref=dst, send_sem=send, recv_sem=recv, device_id=dev, device_id_type=MESH
        )

    barrier = pltpu.get_barrier_semaphore()
    for o in range(1, 16):
        pl.semaphore_signal(barrier, inc=1, device_id=(dp_peer(o), sec), device_id_type=MESH)
    for dev in (x_peer(1), x_peer(2), x_peer(3), z_peer(1), z_peer(2)):
        pl.semaphore_signal(barrier, inc=1, device_id=dev, device_id_type=MESH)

    def section_columns(p):
        return pl.ds(pl.multiple_of(p * columns, columns), columns)

    def features(side, j):
        return pl.ds(pl.multiple_of(side * half + j * FEATURES, FEATURES), FEATURES)

    def lanes(t):
        return pl.ds(t * FEATURES, FEATURES)

    def own_copy(j, t):
        w = (kw_hbm, vw_hbm)[t]
        return pltpu.make_async_copy(w.at[0, :, features(zl, j)], W.at[j, y, zl, c, :, lanes(t)], own_sem.at[j, t])

    def q_own(j, t):
        q = (q_hbm, g_hbm)[t]
        return pltpu.make_async_copy(q.at[0, :, features(zl, j)], QG.at[j, zl, :, lanes(t)], q_own_sem.at[j, t])

    up_columns = pl.ds(pl.multiple_of(zl * half, half), half)
    local = [
        pltpu.make_async_copy(enc_hbm, E.at[zl, :, section_columns(sec)], local_sem.at[0]),
        pltpu.make_async_copy(kd_hbm, down.at[0:16], local_sem.at[1]),
        pltpu.make_async_copy(vd_hbm, down.at[16:32], local_sem.at[2]),
        pltpu.make_async_copy(ku_hbm.at[0, :, up_columns], up.at[0], local_sem.at[3]),
        pltpu.make_async_copy(vu_hbm.at[0, :, up_columns], up.at[1], local_sem.at[4]),
    ]
    for j in range(chunks):
        for t in range(2):
            own_copy(j, t).start()
    for copy in local:
        copy.start()
    for j in range(chunks):
        for t in range(2):
            q_own(j, t).start()
    lens[zl] = jnp.full(lens.shape[1:], len_ref[0], jnp.int32)
    A[...] = jnp.zeros(A.shape, BF16)
    pl.semaphore_wait(barrier, 20)

    def pair(j, y_, c_):
        return W.at[j, y_, :, c_]

    def w_copy(j, n, dev, ref):
        return remote(ref, ref, w_send.at[j, n], w_recv.at[j, n], dev)

    def w_out(j, n):
        if n in (0, 9):
            t = 0 if n == 0 else 1
            w = (kw_hbm, vw_hbm)[t]
            return remote(
                w.at[0, :, features(1 - zl, j)], W.at[j, y, zl, c, :, lanes(t)], w_send.at[j, n], w_recv.at[j, n], ZM
            )
        if n in (1, 2):
            return w_copy(j, n, UP if n == 1 else DN, pair(j, y, c))
        if n == 3:
            return w_copy(j, n, UP, W.at[j, ym, 0, c])
        if n == 4:
            return w_copy(j, n, DN, W.at[j, yp, 1, c])
        return w_copy(j, n, CM, pair(j, (y, ym, yp, yo)[n - 5], c))

    def w_in(j, n):
        if n in (0, 9):
            return w_copy(j, n, ZM, W.at[j, y, 1 - zl, c, :, lanes(0 if n == 0 else 1)])
        if n in (1, 2):
            return w_copy(j, n, DN if n == 1 else UP, pair(j, ym if n == 1 else yp, c))
        if n in (3, 4):
            return w_copy(j, n, DN if n == 3 else UP, W.at[j, yo, n - 3, c])
        return w_copy(j, n, CM, pair(j, (y, ym, yp, yo)[n - 5], 1 - c))

    def go(j, *ns):
        for n in ns:
            w_out(j, n).start()

    def wt(j, *ns):
        for n in ns:
            w_in(j, n).wait_recv()

    def st1(j):
        go(j, 0, 9)

    def st2(j):
        for t in range(2):
            own_copy(j, t).wait()
        wt(j, 0, 9)
        go(j, 1, 2, 5)

    def st3(j):
        wt(j, 1, 2)
        go(j, 3, 4, 6, 7)

    def st4(j):
        wt(j, 3, 4)
        go(j, 8)

    def st5(j):
        wt(j, 5, 6, 7, 8)

    def q_out(j, t):
        q = (q_hbm, g_hbm)[t]
        return remote(
            q.at[0, :, features(1 - zl, j)], QG.at[j, zl, :, lanes(t)], q_send.at[j, t], q_recv.at[j, t], ZM
        )

    def q_in(j, t):
        ref = QG.at[j, 1 - zl, :, lanes(t)]
        return remote(ref, ref, q_send.at[j, t], q_recv.at[j, t], ZM)

    def send_q(j):
        for t in range(2):
            q_out(j, t).start()

    def e_piece(s, p):
        return E.at[s, :, section_columns(p)]

    def ez_out(a):
        return remote(enc_hbm, e_piece(zl, sec), ez_send.at[a], ez_recv.at[a], z_peer(a))

    def ez_in(a):
        z_, h_ = z_coords[a]
        ref = e_piece(z_, x * 2 + h_)
        return remote(ref, ref, ez_send.at[a], ez_recv.at[a], z_peer(a))

    def ex_out(d, k):
        dev = x_peer(1 if d == 0 else 3)
        if k == 0:
            return remote(enc_hbm, e_piece(zl, sec), ex_send.at[d, k], ex_recv.at[d, k], dev)
        z_, h_ = z_coords[k - 1]
        ref = e_piece(z_, x * 2 + h_)
        return remote(ref, ref, ex_send.at[d, k], ex_recv.at[d, k], dev)

    def ex_in(d, m, s):
        k = 2 * m + jnp.where(s == zl, 0, 1)
        ref = e_piece(s, sec_of(3 if d == 0 else 1, 1 - zh if m else zh))
        return remote(ref, ref, ex_send.at[d, k], ex_recv.at[d, k], x_peer(3 if d == 0 else 1))

    def ef_out(d, m):
        ref = e_piece(d, sec_of(3 if d == 0 else 1, 1 - zh if m else zh))
        return remote(ref, ref, ef_send.at[d, m], ef_recv.at[d, m], x_peer(1 if d == 0 else 3))

    def ef_in(d, m):
        ref = e_piece(d, sec_of(2, 1 - zh if m else zh))
        return remote(ref, ref, ef_send.at[d, m], ef_recv.at[d, m], x_peer(3 if d == 0 else 1))

    def e_second():
        for a in range(3):
            ez_in(a).wait_recv()
            for d in range(2):
                ex_out(d, a + 1).start()

    def e_third():
        for m in range(2):
            for d in range(2):
                ex_in(d, m, d).wait_recv()
                ef_out(d, m).start()

    def len_copy(s):
        return remote(lens.at[s], lens.at[s], len_send.at[0], len_recv.at[0], ZM)

    st1(0)
    for a in range(3):
        ez_out(a).start()
    for d in range(2):
        ex_out(d, 0).start()
    len_copy(zl).start()

    def first():
        for copy in local:
            copy.wait()
        len_copy(1 - zl).wait_recv()
        for m in range(2):
            for d in range(2):
                ex_in(d, m, 1 - d).wait_recv()
                ef_in(d, m).wait_recv()
        states = E[...].reshape(2 * BLOCK, E.shape[2])
        low[...] = dot_nt(states, down[...]).astype(BF16)
        low_t[...] = dot_nt(down[...], states).astype(BF16)
        lowg[...] = jnp.zeros(lowg.shape, F32)
        up_pack[...] = jnp.zeros(up_pack.shape, BF16)
        for j in range(chunks):
            for t in range(2):
                up_pack[j, 16 * t : 16 * t + 16, FEATURES * t : FEATURES * t + FEATURES] = up[
                    t, :, FEATURES * j : FEATURES * j + FEATURES
                ]

    def compute(j):
        for t in range(2):
            q_own(j, t).wait()
            q_in(j, t).wait_recv()
        weight = W[j].reshape(16 * BLOCK, PACK)
        base = dot(E[...].reshape(2 * BLOCK, E.shape[2]), weight)
        base = base + adapter_scale * dot(low[...], up_pack[j])
        rows = base.astype(BF16)
        lane = lax.broadcasted_iota(jnp.int32, (1, FEATURES), 1) // HEAD_DIM
        index = lax.broadcasted_iota(jnp.int32, (BLOCK, 1), 0)
        zero = jnp.zeros((), BF16)
        grads = []
        for s in range(2):
            visible = index < lens[s, 0:1, 0:1]
            key_rows = rows[BLOCK * s : BLOCK * s + BLOCK, :FEATURES]
            value_rows = rows[BLOCK * s : BLOCK * s + BLOCK, FEATURES:]
            q, g = QG[j, s, :, :FEATURES], QG[j, s, :, FEATURES:]
            dkeys = jnp.zeros((BLOCK, FEATURES), F32)
            dvalues = jnp.zeros((BLOCK, FEATURES), F32)
            for h in range(FEATURES // HEAD_DIM):
                here = lane == h
                scores = dot_nt(jnp.where(here, key_rows, zero), q)
                scores = jnp.where(visible, scores, masked_score)
                expo = jnp.exp(scores - jnp.max(scores, axis=0, keepdims=True))
                probs = (expo * (1.0 / jnp.sum(expo, axis=0, keepdims=True))).astype(BF16)
                dprobs = dot_nt(jnp.where(here, value_rows, zero), g)
                wide = probs.astype(F32)
                inner = jnp.sum(wide * dprobs, axis=0, keepdims=True)
                dscores = (wide * (dprobs - inner)).astype(BF16)
                dvalues = jnp.where(here, dot(probs, g), dvalues)
                dkeys = jnp.where(here, dot(dscores, q), dkeys)
            grads.append(jnp.concatenate([dkeys, dvalues], axis=1).astype(BF16))
        grad = jnp.concatenate(grads, axis=0)
        dkv[:, pl.ds(pl.multiple_of(j * PACK, PACK), PACK)] = grad
        lowg[...] += dot_nt(grad, up_pack[j])
        up_grad = adapter_scale * dot(low_t[...], grad)
        r = ((j // 2) * 2 + zl) * 2 + lax.rem(j, 2)
        for t in range(2):
            A[r, pl.ds(16 * t, 16), 256:384] = up_grad[
                16 * t : 16 * t + 16, FEATURES * t : FEATURES * t + FEATURES
            ].astype(BF16)

    def within(j, fn):
        @pl.when(jnp.logical_and(j >= 0, j < chunks))
        def _():
            fn(j)

    def slot(k, carry):
        within(k + 1, st1)
        within(k, st2)

        @pl.when(k == 0)
        def _():
            e_second()

        within(k - 1, send_q)
        within(k - 1, st3)

        @pl.when(k == 3)
        def _():
            e_third()

        within(k - 2, st4)
        within(k - 3, st5)

        @pl.when(k == 3)
        def _():
            first()

        within(k - 3, compute)
        return carry

    lax.fori_loop(0, chunks + 3, slot, 0)

    scaled = adapter_scale * lowg[...]
    low[...] = scaled.astype(BF16)
    both = scaled.T.astype(BF16)

    def down_grad(r, carry):
        e = E[:, :, pl.ds(pl.multiple_of(r * BLOCK, BLOCK), BLOCK)].reshape(2 * BLOCK, BLOCK)
        A[r, :, 0:256] = dot(both, e).astype(BF16)
        return carry

    lax.fori_loop(0, 16, down_grad, 0, unroll=4)

    def reduce_copy(o):
        return remote(A.at[dp_peer(o)], A_recv.at[o], r_send.at[o], r_recv.at[o], (dp_peer(o), sec))

    for o in range(1, 16):
        reduce_copy(o).start()

    def back_place(i):
        dx = jnp.where(i < 2, 2, jnp.where(i < 6, 1 + 2 * lax.rem(i, 2), 0))
        other = jnp.where(i < 2, 1 - i, jnp.where(i < 6, 1 - (i - 2) // 2, 7 - i))
        return dx, other

    def z_first_copy(a):
        s = z_coords[a][0]
        i = 1 if a == 0 else 0
        return remote(stage.at[i, s], z_first.at[a], zf_send.at[a], zf_recv.at[a], z_peer(a))

    def x_part_copy(d, e, s):
        i = (4 if e == 0 else 2) + d
        return remote(stage.at[i, s], x_part.at[d, e, s], xp_send.at[d, e, s], xp_recv.at[d, e, s], x_peer(1 if d == 0 else 3))

    def z_part_copy(a):
        return remote(z_sum.at[a], z_part.at[a], zp_send.at[a], zp_recv.at[a], z_peer(a))

    def far_copy():
        return remote(z_first_sum, x_far, far_send.at[0], far_recv.at[0], x_peer(2))

    def back(i, carry):
        dx, other = back_place(i)
        p = lax.rem(x + dx, 4) * 2 + jnp.where(other == 1, 1 - zh, zh)
        for b in range(2):
            r = 2 * p + b
            r_y, r_z, r_c = r // 4, lax.rem(r // 2, 2), lax.rem(r, 2)
            wide = jnp.concatenate([W[j, r_y, r_z, r_c] for j in range(chunks)], axis=1)
            acc = dot_nt(dkv[...], wide)
            acc = acc + dot(low[...], down[:, pl.ds(pl.multiple_of(r * BLOCK, BLOCK), BLOCK)])
            stage[i, :, :, b * BLOCK : (b + 1) * BLOCK] = acc.astype(BF16).reshape(2, BLOCK, BLOCK)

        @pl.when(i == 0)
        def _():
            z_first_copy(2).start()
            z_first_copy(1).start()

        @pl.when(i == 1)
        def _():
            z_first_copy(0).start()

        for d in range(2):
            for e in range(2):

                @pl.when(i == (4 if e == 0 else 2) + d)
                def _(d=d, e=e):
                    x_part_copy(d, e, 1 - zl).start()
                    x_part_copy(d, e, zl).start()

        return carry

    lax.fori_loop(0, 8, back, 0)

    total = stage[1, zl].astype(F32)
    for a in range(3):
        z_first_copy(a).wait_recv()
        total = total + z_first[a].astype(F32)
    z_first_sum[...] = total.astype(BF16)
    far_copy().start()

    def drain(j, carry):
        for n in range(10):
            w_out(j, n).wait_send()
        for t in range(2):
            q_out(j, t).wait_send()
        return carry

    lax.fori_loop(0, chunks, drain, 0)
    for a in range(3):
        ez_out(a).wait_send()
    for d in range(2):
        for k in range(4):
            ex_out(d, k).wait_send()
        for m in range(2):
            ef_out(d, m).wait_send()
    len_copy(zl).wait_send()

    total = A[dp].astype(F32)
    for o in range(1, 16):
        reduce_copy(o).wait_recv()
        total = total + A_recv[o].astype(F32)
    A_all[dp] = total

    def spread_copy(o, index):
        return remote(A_all.at[index], A_all.at[index], a_send.at[o], a_recv.at[o], (dp_peer(o), sec))

    for o in range(1, 16):
        spread_copy(o, dp).start()

    def over_x(e, s):
        sum_ = stage[7 - e, s].astype(F32)
        for d in range(2):
            x_part_copy(d, e, s).wait_recv()
            sum_ = sum_ + x_part[d, e, s].astype(F32)
        return sum_

    for a in (2, 1, 0):
        z_sum[a] = over_x(0 if a == 0 else 1, z_coords[a][0]).astype(BF16)
        z_part_copy(a).start()

    for o in range(1, 16):
        spread_copy(o, lax.rem(dp + 16 - o, 16)).wait_recv()
    for r in range(16):
        first_up = r // 2 % 2 * half + (r // 4 * 2 + r % 2) * FEATURES
        kd_ref[:, r * 256 : r * 256 + 256] = A_all[r, 0:16, 0:256]
        vd_ref[:, r * 256 : r * 256 + 256] = A_all[r, 16:32, 0:256]
        ku_ref[:, pl.ds(first_up, FEATURES)] = A_all[r, 0:16, 256:384]
        vu_ref[:, pl.ds(first_up, FEATURES)] = A_all[r, 16:32, 256:384]

    total = over_x(0, zl)
    far_copy().wait_recv()
    total = total + x_far[...].astype(F32)
    for a in (2, 1, 0):
        z_part_copy(a).wait_recv()
        total = total + z_part[a].astype(F32)
    out_ref[...] = total.astype(BF16)

    for a in range(3):
        z_first_copy(a).wait_send()
        z_part_copy(a).wait_send()
    for d in range(2):
        for e in range(2):
            for s in range(2):
                x_part_copy(d, e, s).wait_send()
    far_copy().wait_send()
    for o in range(1, 16):
        reduce_copy(o).wait_send()
        spread_copy(o, dp).wait_send()


def settle(*refs):
    sem = refs[-1]
    copies = [pltpu.make_async_copy(refs[i], refs[5 + i], sem.at[i]) for i in range(5)]
    for copy in copies:
        copy.start()
    for copy in copies:
        copy.wait()


def per_device(
    enc_states, queries, cotangent, enc_lengths, key_weight, value_weight, key_down, key_up, value_down, value_up
):
    inner = queries.shape[2]
    chunks = inner // 2 // FEATURES
    width = key_down.shape[1]
    columns = enc_states.shape[1]
    rows = queries.shape[1]
    hbm = pl.BlockSpec(memory_space=pl.ANY)
    vmem = pl.BlockSpec(memory_space=pltpu.VMEM)
    dma = pltpu.SemaphoreType.DMA
    piece = (BLOCK, columns)
    results = pl.pallas_call(
        functools.partial(kernel, chunks),
        out_shape=(
            jax.ShapeDtypeStruct((BLOCK, columns), BF16),
            jax.ShapeDtypeStruct((16, width), F32),
            jax.ShapeDtypeStruct((16, inner), F32),
            jax.ShapeDtypeStruct((16, width), F32),
            jax.ShapeDtypeStruct((16, inner), F32),
        ),
        in_specs=[hbm, hbm, hbm, pl.BlockSpec(memory_space=pltpu.SMEM)] + [hbm] * 6,
        out_specs=(vmem,) * 5,
        scratch_shapes=[
            pltpu.VMEM((chunks, 4, 2, 2, BLOCK, PACK), BF16),
            pltpu.VMEM((2, BLOCK, width), BF16),
            pltpu.VMEM((chunks, 2, rows, PACK), BF16),
            pltpu.VMEM((2, 8, 128), jnp.int32),
            pltpu.VMEM((32, width), BF16),
            pltpu.VMEM((2, 16, inner // 2), BF16),
            pltpu.VMEM((chunks, 32, PACK), BF16),
            pltpu.VMEM((2 * BLOCK, 32), BF16),
            pltpu.VMEM((32, 2 * BLOCK), BF16),
            pltpu.VMEM((2 * BLOCK, 32), F32),
            pltpu.VMEM((2 * BLOCK, chunks * PACK), BF16),
            pltpu.VMEM((8, 2) + piece, BF16),
            pltpu.VMEM((2, 2, 2) + piece, BF16),
            pltpu.VMEM((3,) + piece, BF16),
            pltpu.VMEM(piece, BF16),
            pltpu.VMEM((3,) + piece, BF16),
            pltpu.VMEM((3,) + piece, BF16),
            pltpu.VMEM(piece, BF16),
            pltpu.VMEM((16, 32, 384), BF16),
            pltpu.VMEM((16, 32, 384), BF16),
            pltpu.VMEM((16, 32, 384), F32),
            dma((5,)),
            dma((chunks, 2)),
            dma((chunks, 2)),
            dma((chunks, 10)),
            dma((chunks, 10)),
            dma((chunks, 2)),
            dma((chunks, 2)),
            dma((3,)),
            dma((3,)),
            dma((2, 4)),
            dma((2, 4)),
            dma((2, 2)),
            dma((2, 2)),
            dma((1,)),
            dma((1,)),
            dma((3,)),
            dma((3,)),
            dma((2, 2, 2)),
            dma((2, 2, 2)),
            dma((3,)),
            dma((3,)),
            dma((1,)),
            dma((1,)),
            dma((16,)),
            dma((16,)),
            dma((16,)),
            dma((16,)),
        ],
        compiler_params=pltpu.CompilerParams(
            collective_id=0, has_side_effects=True, vmem_limit_bytes=60 * 1024 * 1024
        ),
        name="adapter_backward",
    )(
        enc_states, queries, cotangent, enc_lengths, key_weight, value_weight,
        key_down[0].T, key_up, value_down[0].T, value_up,
    )
    out, kd_grad, ku_grad, vd_grad, vu_grad = pl.pallas_call(
        settle,
        out_shape=tuple(jax.ShapeDtypeStruct(r.shape, r.dtype) for r in results),
        in_specs=[vmem] * 5,
        out_specs=(hbm,) * 5,
        scratch_shapes=[dma((5,))],
        name="results",
    )(*results)
    return out, kd_grad.T[None], ku_grad[None], vd_grad.T[None], vu_grad[None]


def solution(mesh):
    return jax.shard_map(
        per_device,
        mesh=mesh,
        in_specs=(
            P("dp", "section"),
            P("section", "dp", None),
            P("section", "dp", None),
            P("dp"),
            P("section", "dp", None),
            P("section", "dp", None),
            P("section", None, None),
            P("section", None, None),
            P("section", None, None),
            P("section", None, None),
        ),
        out_specs=(
            P("dp", "section"),
            P("section", None, None),
            P("section", None, None),
            P("section", None, None),
            P("section", None, None),
        ),
        check_vma=False,
    )
```

time: 587 us -> 152 us (0.26)
  waiting for transfers between devices: 459 us -> 0 us
  Pallas kernels: 0 us -> 150 us
  matrix products: 89.6 us -> 0 us
  between operations: 14.6 us -> 1.29 us
  local copies, waits for them, and re-layouts: 12.3 us -> 0 us
  other arithmetic: 11 us -> 0 us
    all_gather x3 -> x0, waiting for transfers between devices: 229 us -> none  [the longest x1 88.7 us: per_device(): lax.all_gather(key_weight, 'dp', axis=1, tiled=True)]
    psum x2 -> x0, waiting for transfers between devices: 228 us -> none  [the longest x1 123 us: per_device(): lax.psum((key_down_grad, key_up_grad, value_down_grad, value_up_grad), 'dp')]
    pallas_call x0 -> x2, Pallas kernels: none -> 150 us  [the longest x1 148 us: per_device(): pl.pallas_call(functools.partial(kernel, chunks), out_shape=(jax.ShapeDty...]
    dot_general x19 -> x0, matrix products: 78.5 us -> none  [the longest x2 23.1 us: adapter_back(): through = jnp.dot(gradient, weight.T, preferred_element_type=jnp.float32)]
    sub x1 -> x0, matrix products: 11 us -> none  [per_device(): expo = jnp.exp(scores - peak_score)]
    convert_element_type x2 -> x0, other arithmetic: 10.5 us -> none  [the longest x1 8.83 us: per_device(): probs = (expo / jnp.sum(expo, axis=2, keepdims=True)).astype(jnp.bfloat16)]
    unnamed x28 -> x0, local copies, waits for them, and re-layouts: 9.72 us -> none
  transfers between devices with their start and end apart: 5 -> 0, of which waited for: 5 -> 0; matrix products, arithmetic and copies ran while one was open for 4% -> 0% of each run, Pallas kernels for 0% -> 0%
where the time goes in v3:
time: 152 us
  Pallas kernels  150 us (99%)
    pallas_call x1, Pallas kernels, per_device(): pl.pallas_call(functools.partial(kernel, chunks), out_shape=(jax.ShapeDty...  148 us

profile of v3, /device:TPU:1, one launch (start us, length us, event | category | flops | bytes accessed | tf_op | source)
XLA Modules:
  0.0 151.6 jit_solution(6646381324240901031)
XLA Ops:
  1.3 148.2 %adapter_backward.1 = (bf16[256,512]{1,0:T(8,128)(2,1)}, f32[16,4096]{1,0:T(8,128)}, f32[16,2048]{1,0:T(8,128)}, f32[16,4096]{1,0:T(8,128)}, f32[16,2048]{1,0:T(8,128)}) custom-call(bf16[256,512]{1,0:T(8,128)(2,1)} %enc_hbm.1, bf16[1,384,2048]{2,1,0:T(8,128)(2,1)} %q_hbm.1, bf16[1,384,2048]{2,1,0:T(8,128)(2,1)} %g_hbm.1, s32[1]{0:T(128)S(6)} %copy.15.len_ref, ...), custom_call_target="tpu_custom_call" | custom-call | tf_op jit(solution)/shard_map/adapter_backward/pallas_call | solution.py:506
  149.5 2.2 %results.1 = (bf16[256,512]{1,0:T(8,128)(2,1)}, f32[16,4096]{1,0:T(8,128)}, f32[16,2048]{1,0:T(8,128)}, f32[16,4096]{1,0:T(8,128)}, f32[16,2048]{1,0:T(8,128)}) custom-call(bf16[256,512]{1,0:T(8,128)(2,1)} %get-tuple-element.15.refs_0_, f32[16,4096]{1,0:T(8,128)} %get-tuple-element.16.refs_1_, f32[16,2048]{1,0:T(8,128)} %get-tuple-element.17.refs_2_, ...), custom_call_target="tpu_custom_call" | custom-call | tf_op jit(solution)/shard_map/results/pallas_call | solution.py:575

commit v4 on v3

--- a/solution.py
+++ b/solution.py
@@ -35,7 +35,7 @@
     out_ref, kd_ref, ku_ref, vd_ref, vu_ref,
     W, E, QG, lens, down, up, up_pack, low, low_t, lowg, dkv,
     stage, x_part, z_first, z_first_sum, z_sum, z_part, x_far,
-    A, A_recv, A_all,
+    A, A_core, A_sum, A_recv, A_all,
     local_sem, own_sem, q_own_sem, w_send, w_recv, q_send, q_recv,
     ez_send, ez_recv, ex_send, ex_recv, ef_send, ef_recv, len_send, len_recv,
     zf_send, zf_recv, xp_send, xp_recv, zp_send, zp_recv, far_send, far_recv,
@@ -54,8 +54,13 @@
 
     UP, DN, ZM, CM = did(yp, zl, c), did(ym, zl, c), did(y, 1 - zl, c), did(y, zl, 1 - c)
 
-    def dp_peer(o):
-        return lax.rem(dp + o, 16)
+    me = dp // 2
+
+    def chip(o):
+        return lax.rem(me + o, 8)
+
+    def chip_device(o):
+        return (chip(o) * 2 + c, sec)
 
     def sec_of(dx, zh_):
         return lax.rem(x + dx, 4) * 2 + zh_
@@ -75,9 +80,9 @@
         )
 
     barrier = pltpu.get_barrier_semaphore()
-    for o in range(1, 16):
-        pl.semaphore_signal(barrier, inc=1, device_id=(dp_peer(o), sec), device_id_type=MESH)
-    for dev in (x_peer(1), x_peer(2), x_peer(3), z_peer(1), z_peer(2)):
+    for o in range(1, 8):
+        pl.semaphore_signal(barrier, inc=1, device_id=chip_device(o), device_id_type=MESH)
+    for dev in (CM, x_peer(1), x_peer(2), x_peer(3), z_peer(1), z_peer(2)):
         pl.semaphore_signal(barrier, inc=1, device_id=dev, device_id_type=MESH)
 
     def section_columns(p):
@@ -115,7 +120,7 @@
             q_own(j, t).start()
     lens[zl] = jnp.full(lens.shape[1:], len_ref[0], jnp.int32)
     A[...] = jnp.zeros(A.shape, BF16)
-    pl.semaphore_wait(barrier, 20)
+    pl.semaphore_wait(barrier, 13)
 
     def pair(j, y_, c_):
         return W.at[j, y_, :, c_]
@@ -130,8 +135,15 @@
             return remote(
                 w.at[0, :, features(1 - zl, j)], W.at[j, y, zl, c, :, lanes(t)], w_send.at[j, n], w_recv.at[j, n], ZM
             )
-        if n in (1, 2):
-            return w_copy(j, n, UP if n == 1 else DN, pair(j, y, c))
+        if n in (1, 2, 10, 11):
+            t = 0 if n in (1, 2) else 1
+            w = (kw_hbm, vw_hbm)[t]
+            return remote(
+                w.at[0, :, features(zl, j)], W.at[j, y, zl, c, :, lanes(t)], w_send.at[j, n], w_recv.at[j, n],
+                UP if n in (1, 10) else DN,
+            )
+        if n in (12, 13):
+            return w_copy(j, n, UP if n == 12 else DN, W.at[j, y, 1 - zl, c])
         if n == 3:
             return w_copy(j, n, UP, W.at[j, ym, 0, c])
         if n == 4:
@@ -141,8 +153,12 @@
     def w_in(j, n):
         if n in (0, 9):
             return w_copy(j, n, ZM, W.at[j, y, 1 - zl, c, :, lanes(0 if n == 0 else 1)])
-        if n in (1, 2):
-            return w_copy(j, n, DN if n == 1 else UP, pair(j, ym if n == 1 else yp, c))
+        if n in (1, 2, 10, 11):
+            up_ = n in (1, 10)
+            t = 0 if n in (1, 2) else 1
+            return w_copy(j, n, DN if up_ else UP, W.at[j, ym if up_ else yp, zl, c, :, lanes(t)])
+        if n in (12, 13):
+            return w_copy(j, n, DN if n == 12 else UP, W.at[j, ym if n == 12 else yp, 1 - zl, c])
         if n in (3, 4):
             return w_copy(j, n, DN if n == 3 else UP, W.at[j, yo, n - 3, c])
         return w_copy(j, n, CM, pair(j, (y, ym, yp, yo)[n - 5], 1 - c))
@@ -156,16 +172,16 @@
             w_in(j, n).wait_recv()
 
     def st1(j):
-        go(j, 0, 9)
+        go(j, 0, 9, 1, 2, 10, 11)
 
     def st2(j):
         for t in range(2):
             own_copy(j, t).wait()
         wt(j, 0, 9)
-        go(j, 1, 2, 5)
+        go(j, 12, 13, 5)
 
     def st3(j):
-        wt(j, 1, 2)
+        wt(j, 1, 2, 10, 11, 12, 13)
         go(j, 3, 4, 6, 7)
 
     def st4(j):
@@ -237,6 +253,7 @@
         return remote(lens.at[s], lens.at[s], len_send.at[0], len_recv.at[0], ZM)
 
     st1(0)
+    st1(1)
     for a in range(3):
         ez_out(a).start()
     for d in range(2):
@@ -269,38 +286,44 @@
         weight = W[j].reshape(16 * BLOCK, PACK)
         base = dot(E[...].reshape(2 * BLOCK, E.shape[2]), weight)
         base = base + adapter_scale * dot(low[...], up_pack[j])
-        rows = base.astype(BF16)
+        here_columns = pl.ds(pl.multiple_of(j * PACK, PACK), PACK)
+        dkv[:, here_columns] = base.astype(BF16)
         lane = lax.broadcasted_iota(jnp.int32, (1, FEATURES), 1) // HEAD_DIM
         index = lax.broadcasted_iota(jnp.int32, (BLOCK, 1), 0)
         zero = jnp.zeros((), BF16)
-        grads = []
-        for s in range(2):
+
+        def sequence(s, carry):
+            here_rows = pl.ds(pl.multiple_of(s * BLOCK, BLOCK), BLOCK)
+            rows = dkv[here_rows, here_columns]
+            key_rows, value_rows = rows[:, :FEATURES], rows[:, FEATURES:]
+            q, g = QG[j, s, :, :FEATURES], QG[j, s, :, FEATURES:]
             visible = index < lens[s, 0:1, 0:1]
-            key_rows = rows[BLOCK * s : BLOCK * s + BLOCK, :FEATURES]
-            value_rows = rows[BLOCK * s : BLOCK * s + BLOCK, FEATURES:]
-            q, g = QG[j, s, :, :FEATURES], QG[j, s, :, FEATURES:]
-            dkeys = jnp.zeros((BLOCK, FEATURES), F32)
-            dvalues = jnp.zeros((BLOCK, FEATURES), F32)
-            for h in range(FEATURES // HEAD_DIM):
-                here = lane == h
-                scores = dot_nt(jnp.where(here, key_rows, zero), q)
-                scores = jnp.where(visible, scores, masked_score)
-                expo = jnp.exp(scores - jnp.max(scores, axis=0, keepdims=True))
+            scores = dot_nt(jnp.concatenate([jnp.where(lane == h, key_rows, zero) for h in range(2)], axis=0), q)
+            dprobs = dot_nt(jnp.concatenate([jnp.where(lane == h, value_rows, zero) for h in range(2)], axis=0), g)
+            all_probs, all_dscores = [], []
+            for h in range(2):
+                masked = jnp.where(visible, scores[BLOCK * h : BLOCK * h + BLOCK], masked_score)
+                expo = jnp.exp(masked - jnp.max(masked, axis=0, keepdims=True))
                 probs = (expo * (1.0 / jnp.sum(expo, axis=0, keepdims=True))).astype(BF16)
-                dprobs = dot_nt(jnp.where(here, value_rows, zero), g)
                 wide = probs.astype(F32)
-                inner = jnp.sum(wide * dprobs, axis=0, keepdims=True)
-                dscores = (wide * (dprobs - inner)).astype(BF16)
-                dvalues = jnp.where(here, dot(probs, g), dvalues)
-                dkeys = jnp.where(here, dot(dscores, q), dkeys)
-            grads.append(jnp.concatenate([dkeys, dvalues], axis=1).astype(BF16))
-        grad = jnp.concatenate(grads, axis=0)
-        dkv[:, pl.ds(pl.multiple_of(j * PACK, PACK), PACK)] = grad
+                dprob = dprobs[BLOCK * h : BLOCK * h + BLOCK]
+                inner = jnp.sum(wide * dprob, axis=0, keepdims=True)
+                all_probs.append(probs)
+                all_dscores.append((wide * (dprob - inner)).astype(BF16))
+            dvalues = dot(jnp.concatenate(all_probs, axis=0), g)
+            dkeys = dot(jnp.concatenate(all_dscores, axis=0), q)
+            both = [jnp.where(lane == 0, d[:BLOCK], d[BLOCK:]) for d in (dkeys, dvalues)]
+            dkv[here_rows, here_columns] = jnp.concatenate(both, axis=1).astype(BF16)
+            return carry
+
+        lax.fori_loop(0, 2, sequence, 0)
+        grad = dkv[:, here_columns]
         lowg[...] += dot_nt(grad, up_pack[j])
         up_grad = adapter_scale * dot(low_t[...], grad)
-        r = ((j // 2) * 2 + zl) * 2 + lax.rem(j, 2)
+        r = (j // 2) * 2 + zl
+        r_core = lax.rem(j, 2)
         for t in range(2):
-            A[r, pl.ds(16 * t, 16), 256:384] = up_grad[
+            A[r, r_core, pl.ds(16 * t, 16), 256:384] = up_grad[
                 16 * t : 16 * t + 16, FEATURES * t : FEATURES * t + FEATURES
             ].astype(BF16)
 
@@ -309,62 +332,104 @@
         def _():
             fn(j)
 
-    def slot(k, carry):
-        within(k + 1, st1)
-        within(k, st2)
-
-        @pl.when(k == 0)
-        def _():
-            e_second()
-
-        within(k - 1, send_q)
-        within(k - 1, st3)
-
-        @pl.when(k == 3)
-        def _():
-            e_third()
-
-        within(k - 2, st4)
-        within(k - 3, st5)
-
-        @pl.when(k == 3)
-        def _():
-            first()
-
-        within(k - 3, compute)
+    computed = (10, 12, 13, 14, 15, 17, 19, 21)
+
+    def half_slot(i, carry):
+        k = i // 2
+
+        @pl.when(lax.rem(i, 2) == 0)
+        def _():
+            within(k + 2, st1)
+            within(k, st2)
+
+            @pl.when(k == 5)
+            def _():
+                first()
+
+        @pl.when(lax.rem(i, 2) == 1)
+        def _():
+            within(k - 1, send_q)
+            within(k - 1, st3)
+
+            @pl.when(k == 1)
+            def _():
+                e_second()
+
+            @pl.when(k == 2)
+            def _():
+                e_third()
+
+            within(k - 2, st4)
+            within(k - 3, st5)
+
+        now = i == computed[0]
+        j = jnp.int32(0)
+        for at in computed[1:]:
+            now = jnp.logical_or(now, i == at)
+            j = j + jnp.where(i >= at, 1, 0)
+
+        @pl.when(now)
+        def _():
+            compute(j)
+
         return carry
 
-    lax.fori_loop(0, chunks + 3, slot, 0)
-
-    scaled = adapter_scale * lowg[...]
-    low[...] = scaled.astype(BF16)
-    both = scaled.T.astype(BF16)
-
-    def down_grad(r, carry):
-        e = E[:, :, pl.ds(pl.multiple_of(r * BLOCK, BLOCK), BLOCK)].reshape(2 * BLOCK, BLOCK)
-        A[r, :, 0:256] = dot(both, e).astype(BF16)
-        return carry
-
-    lax.fori_loop(0, 16, down_grad, 0, unroll=4)
+    lax.fori_loop(0, 2 * (chunks + 3), half_slot, 0)
+
+    low[...] = (adapter_scale * lowg[...]).astype(BF16)
+
+    def core_copy():
+        return remote(A.at[:, 1 - c], A_core, r_send.at[0], r_recv.at[0], CM)
 
     def reduce_copy(o):
-        return remote(A.at[dp_peer(o)], A_recv.at[o], r_send.at[o], r_recv.at[o], (dp_peer(o), sec))
-
-    for o in range(1, 16):
-        reduce_copy(o).start()
+        return remote(A_sum.at[chip(o)], A_recv.at[o], r_send.at[o], r_recv.at[o], chip_device(o))
+
+    def spread_copy(o, index):
+        return remote(A_all.at[index, c], A_all.at[index, c], a_send.at[o], a_recv.at[o], chip_device(o))
+
+    def return_copy(c_):
+        return remote(A_all.at[:, c_], A_all.at[:, c_], a_send.at[0], a_recv.at[0], CM)
+
+    def adapter_pieces():
+        both = (adapter_scale * lowg[...]).T.astype(BF16)
+
+        def down_grad(m, carry):
+            for c_ in range(2):
+                cols = pl.ds(pl.multiple_of((2 * m + c_) * BLOCK, BLOCK), BLOCK)
+                A[m, c_, :, 0:256] = dot(both, E[:, :, cols].reshape(2 * BLOCK, BLOCK)).astype(BF16)
+            return carry
+
+        lax.fori_loop(0, 8, down_grad, 0, unroll=2)
+        core_copy().start()
+
+    def adapter_chip():
+        core_copy().wait_recv()
+        A_sum[...] = (A[:, c].astype(F32) + A_core[...].astype(F32)).astype(BF16)
+        for o in range(1, 8):
+            reduce_copy(o).start()
+
+    def adapter_sums():
+        sum_ = A_sum[me].astype(F32)
+        for o in range(1, 8):
+            reduce_copy(o).wait_recv()
+            sum_ = sum_ + A_recv[o].astype(F32)
+        A_all[me, c] = sum_
+        for o in range(1, 8):
+            spread_copy(o, me).start()
 
     def back_place(i):
-        dx = jnp.where(i < 2, 2, jnp.where(i < 6, 1 + 2 * lax.rem(i, 2), 0))
-        other = jnp.where(i < 2, 1 - i, jnp.where(i < 6, 1 - (i - 2) // 2, 7 - i))
+        far = jnp.logical_or(i == 2, i == 3)
+        dx = jnp.where(far, 2, jnp.where(i < 6, 1 + 2 * lax.rem(i, 2), 0))
+        other = jnp.where(far, 3 - i, jnp.where(i < 6, 1 - i // 4, 7 - i))
         return dx, other
 
     def z_first_copy(a):
         s = z_coords[a][0]
-        i = 1 if a == 0 else 0
+        i = 3 if a == 0 else 2
         return remote(stage.at[i, s], z_first.at[a], zf_send.at[a], zf_recv.at[a], z_peer(a))
 
     def x_part_copy(d, e, s):
-        i = (4 if e == 0 else 2) + d
+        i = (4 if e == 0 else 0) + d
         return remote(stage.at[i, s], x_part.at[d, e, s], xp_send.at[d, e, s], xp_recv.at[d, e, s], x_peer(1 if d == 0 else 3))
 
     def z_part_copy(a):
@@ -374,6 +439,18 @@
         return remote(z_first_sum, x_far, far_send.at[0], far_recv.at[0], x_peer(2))
 
     def back(i, carry):
+        @pl.when(i == 2)
+        def _():
+            adapter_pieces()
+
+        @pl.when(i == 4)
+        def _():
+            adapter_chip()
+
+        @pl.when(i == 7)
+        def _():
+            adapter_sums()
+
         dx, other = back_place(i)
         p = lax.rem(x + dx, 4) * 2 + jnp.where(other == 1, 1 - zh, zh)
         for b in range(2):
@@ -384,19 +461,19 @@
             acc = acc + dot(low[...], down[:, pl.ds(pl.multiple_of(r * BLOCK, BLOCK), BLOCK)])
             stage[i, :, :, b * BLOCK : (b + 1) * BLOCK] = acc.astype(BF16).reshape(2, BLOCK, BLOCK)
 
-        @pl.when(i == 0)
+        @pl.when(i == 2)
         def _():
             z_first_copy(2).start()
             z_first_copy(1).start()
 
-        @pl.when(i == 1)
+        @pl.when(i == 3)
         def _():
             z_first_copy(0).start()
 
         for d in range(2):
             for e in range(2):
 
-                @pl.when(i == (4 if e == 0 else 2) + d)
+                @pl.when(i == (4 if e == 0 else 0) + d)
                 def _(d=d, e=e):
                     x_part_copy(d, e, 1 - zl).start()
                     x_part_copy(d, e, zl).start()
@@ -405,7 +482,7 @@
 
     lax.fori_loop(0, 8, back, 0)
 
-    total = stage[1, zl].astype(F32)
+    total = stage[3, zl].astype(F32)
     for a in range(3):
         z_first_copy(a).wait_recv()
         total = total + z_first[a].astype(F32)
@@ -413,7 +490,7 @@
     far_copy().start()
 
     def drain(j, carry):
-        for n in range(10):
+        for n in range(14):
             w_out(j, n).wait_send()
         for t in range(2):
             q_out(j, t).wait_send()
@@ -429,18 +506,6 @@
             ef_out(d, m).wait_send()
     len_copy(zl).wait_send()
 
-    total = A[dp].astype(F32)
-    for o in range(1, 16):
-        reduce_copy(o).wait_recv()
-        total = total + A_recv[o].astype(F32)
-    A_all[dp] = total
-
-    def spread_copy(o, index):
-        return remote(A_all.at[index], A_all.at[index], a_send.at[o], a_recv.at[o], (dp_peer(o), sec))
-
-    for o in range(1, 16):
-        spread_copy(o, dp).start()
-
     def over_x(e, s):
         sum_ = stage[7 - e, s].astype(F32)
         for d in range(2):
@@ -452,14 +517,17 @@
         z_sum[a] = over_x(0 if a == 0 else 1, z_coords[a][0]).astype(BF16)
         z_part_copy(a).start()
 
-    for o in range(1, 16):
-        spread_copy(o, lax.rem(dp + 16 - o, 16)).wait_recv()
+    for o in range(1, 8):
+        spread_copy(o, chip(8 - o)).wait_recv()
+    return_copy(c).start()
+
+    return_copy(1 - c).wait_recv()
     for r in range(16):
         first_up = r // 2 % 2 * half + (r // 4 * 2 + r % 2) * FEATURES
-        kd_ref[:, r * 256 : r * 256 + 256] = A_all[r, 0:16, 0:256]
-        vd_ref[:, r * 256 : r * 256 + 256] = A_all[r, 16:32, 0:256]
-        ku_ref[:, pl.ds(first_up, FEATURES)] = A_all[r, 0:16, 256:384]
-        vu_ref[:, pl.ds(first_up, FEATURES)] = A_all[r, 16:32, 256:384]
+        kd_ref[:, r * 256 : r * 256 + 256] = A_all[r // 2, r % 2, 0:16, 0:256]
+        vd_ref[:, r * 256 : r * 256 + 256] = A_all[r // 2, r % 2, 16:32, 0:256]
+        ku_ref[:, pl.ds(first_up, FEATURES)] = A_all[r // 2, r % 2, 0:16, 256:384]
+        vu_ref[:, pl.ds(first_up, FEATURES)] = A_all[r // 2, r % 2, 16:32, 256:384]
 
     total = over_x(0, zl)
     far_copy().wait_recv()
@@ -477,9 +545,11 @@
             for s in range(2):
                 x_part_copy(d, e, s).wait_send()
     far_copy().wait_send()
-    for o in range(1, 16):
+    core_copy().wait_send()
+    for o in range(1, 8):
         reduce_copy(o).wait_send()
-        spread_copy(o, dp).wait_send()
+        spread_copy(o, me).wait_send()
+    return_copy(c).wait_send()
 
 
 def settle(*refs):
@@ -533,14 +603,16 @@
             pltpu.VMEM((3,) + piece, BF16),
             pltpu.VMEM((3,) + piece, BF16),
             pltpu.VMEM(piece, BF16),
-            pltpu.VMEM((16, 32, 384), BF16),
-            pltpu.VMEM((16, 32, 384), BF16),
-            pltpu.VMEM((16, 32, 384), F32),
+            pltpu.VMEM((8, 2, 32, 384), BF16),
+            pltpu.VMEM((8, 32, 384), BF16),
+            pltpu.VMEM((8, 32, 384), BF16),
+            pltpu.VMEM((8, 32, 384), BF16),
+            pltpu.VMEM((8, 2, 32, 384), F32),
             dma((5,)),
             dma((chunks, 2)),
             dma((chunks, 2)),
-            dma((chunks, 10)),
-            dma((chunks, 10)),
+            dma((chunks, 14)),
+            dma((chunks, 14)),
             dma((chunks, 2)),
             dma((chunks, 2)),
             dma((3,)),
@@ -559,10 +631,10 @@
             dma((3,)),
             dma((1,)),
             dma((1,)),
-            dma((16,)),
-            dma((16,)),
-            dma((16,)),
-            dma((16,)),
+            dma((8,)),
+            dma((8,)),
+            dma((8,)),
+            dma((8,)),
         ],
         compiler_params=pltpu.CompilerParams(
             collective_id=0, has_side_effects=True, vmem_limit_bytes=60 * 1024 * 1024

time: 152 us -> 133 us (0.88)
  Pallas kernels: 150 us -> 132 us
    pallas_call x1, Pallas kernels: 148 us -> 130 us  [per_device(): pl.pallas_call(functools.partial(kernel, chunks), out_shape=(jax.ShapeDty...]
where the time goes in v4:
time: 133 us
  Pallas kernels  132 us (99%)
    pallas_call x1, Pallas kernels, per_device(): pl.pallas_call(functools.partial(kernel, chunks), out_shape=(jax.ShapeDty...  130 us

profile of v4, /device:TPU:1, one launch (start us, length us, event | category | flops | bytes accessed | tf_op | source)
XLA Modules:
  0.0 133.1 jit_solution(12302606387561483031)
XLA Ops:
  1.3 129.6 %adapter_backward.1 = (bf16[256,512]{1,0:T(8,128)(2,1)}, f32[16,4096]{1,0:T(8,128)}, f32[16,2048]{1,0:T(8,128)}, f32[16,4096]{1,0:T(8,128)}, f32[16,2048]{1,0:T(8,128)}) custom-call(bf16[256,512]{1,0:T(8,128)(2,1)} %enc_hbm.1, bf16[1,384,2048]{2,1,0:T(8,128)(2,1)} %q_hbm.1, bf16[1,384,2048]{2,1,0:T(8,128)(2,1)} %g_hbm.1, s32[1]{0:T(128)S(6)} %copy.15.len_ref, ...), custom_call_target="tpu_custom_call" | custom-call | tf_op jit(solution)/shard_map/adapter_backward/pallas_call | solution.py:576
  130.9 2.2 %results.1 = (bf16[256,512]{1,0:T(8,128)(2,1)}, f32[16,4096]{1,0:T(8,128)}, f32[16,2048]{1,0:T(8,128)}, f32[16,4096]{1,0:T(8,128)}, f32[16,2048]{1,0:T(8,128)}) custom-call(bf16[256,512]{1,0:T(8,128)(2,1)} %get-tuple-element.15.refs_0_, f32[16,4096]{1,0:T(8,128)} %get-tuple-element.16.refs_1_, f32[16,2048]{1,0:T(8,128)} %get-tuple-element.17.refs_2_, ...), custom_call_target="tpu_custom_call" | custom-call | tf_op jit(solution)/shard_map/results/pallas_call | solution.py:647

commit v5 on v4

--- a/solution.py
+++ b/solution.py
@@ -35,8 +35,8 @@
     out_ref, kd_ref, ku_ref, vd_ref, vu_ref,
     W, E, QG, lens, down, up, up_pack, low, low_t, lowg, dkv,
     stage, x_part, z_first, z_first_sum, z_sum, z_part, x_far,
-    A, A_core, A_sum, A_recv, A_all,
-    local_sem, own_sem, q_own_sem, w_send, w_recv, q_send, q_recv,
+    A, A_core, A_sum, A_recv, A_all, down_out, up_out,
+    local_sem, out_sem, own_sem, q_own_sem, w_send, w_recv, q_send, q_recv,
     ez_send, ez_recv, ex_send, ex_recv, ef_send, ef_recv, len_send, len_recv,
     zf_send, zf_recv, xp_send, xp_recv, zp_send, zp_recv, far_send, far_recv,
     r_send, r_recv, a_send, a_recv,
@@ -110,16 +110,7 @@
         pltpu.make_async_copy(ku_hbm.at[0, :, up_columns], up.at[0], local_sem.at[3]),
         pltpu.make_async_copy(vu_hbm.at[0, :, up_columns], up.at[1], local_sem.at[4]),
     ]
-    for j in range(chunks):
-        for t in range(2):
-            own_copy(j, t).start()
-    for copy in local:
-        copy.start()
-    for j in range(chunks):
-        for t in range(2):
-            q_own(j, t).start()
     lens[zl] = jnp.full(lens.shape[1:], len_ref[0], jnp.int32)
-    A[...] = jnp.zeros(A.shape, BF16)
     pl.semaphore_wait(barrier, 13)
 
     def pair(j, y_, c_):
@@ -237,17 +228,15 @@
         ref = e_piece(d, sec_of(2, 1 - zh if m else zh))
         return remote(ref, ref, ef_send.at[d, m], ef_recv.at[d, m], x_peer(3 if d == 0 else 1))
 
-    def e_second():
-        for a in range(3):
-            ez_in(a).wait_recv()
-            for d in range(2):
-                ex_out(d, a + 1).start()
-
-    def e_third():
-        for m in range(2):
-            for d in range(2):
-                ex_in(d, m, d).wait_recv()
-                ef_out(d, m).start()
+    def e_second(a):
+        ez_in(a).wait_recv()
+        for d in range(2):
+            ex_out(d, a + 1).start()
+
+    def e_third(m):
+        for d in range(2):
+            ex_in(d, m, d).wait_recv()
+            ef_out(d, m).start()
 
     def len_copy(s):
         return remote(lens.at[s], lens.at[s], len_send.at[0], len_recv.at[0], ZM)
@@ -259,6 +248,16 @@
     for d in range(2):
         ex_out(d, 0).start()
     len_copy(zl).start()
+
+    for j in range(chunks):
+        for t in range(2):
+            own_copy(j, t).start()
+    for copy in local:
+        copy.start()
+    for j in range(chunks):
+        for t in range(2):
+            q_own(j, t).start()
+    A[...] = jnp.zeros(A.shape, BF16)
 
     def first():
         for copy in local:
@@ -269,8 +268,9 @@
                 ex_in(d, m, 1 - d).wait_recv()
                 ef_in(d, m).wait_recv()
         states = E[...].reshape(2 * BLOCK, E.shape[2])
-        low[...] = dot_nt(states, down[...]).astype(BF16)
-        low_t[...] = dot_nt(down[...], states).astype(BF16)
+        both = dot_nt(states, down[...])
+        low[...] = both.astype(BF16)
+        low_t[...] = both.T.astype(BF16)
         lowg[...] = jnp.zeros(lowg.shape, F32)
         up_pack[...] = jnp.zeros(up_pack.shape, BF16)
         for j in range(chunks):
@@ -342,25 +342,34 @@
             within(k + 2, st1)
             within(k, st2)
 
-            @pl.when(k == 5)
-            def _():
-                first()
-
         @pl.when(lax.rem(i, 2) == 1)
         def _():
             within(k - 1, send_q)
             within(k - 1, st3)
 
-            @pl.when(k == 1)
-            def _():
-                e_second()
-
-            @pl.when(k == 2)
-            def _():
-                e_third()
-
             within(k - 2, st4)
             within(k - 3, st5)
+
+        @pl.when(i == 2)
+        def _():
+            e_second(2)
+            e_second(0)
+
+        @pl.when(i == 4)
+        def _():
+            e_second(1)
+
+        @pl.when(i == 6)
+        def _():
+            e_third(0)
+
+        @pl.when(i == 7)
+        def _():
+            e_third(1)
+
+        @pl.when(i == 10)
+        def _():
+            first()
 
         now = i == computed[0]
         j = jnp.int32(0)
@@ -413,7 +422,7 @@
         for o in range(1, 8):
             reduce_copy(o).wait_recv()
             sum_ = sum_ + A_recv[o].astype(F32)
-        A_all[me, c] = sum_
+        A_all[me, c] = sum_.astype(BF16)
         for o in range(1, 8):
             spread_copy(o, me).start()
 
@@ -439,17 +448,13 @@
         return remote(z_first_sum, x_far, far_send.at[0], far_recv.at[0], x_peer(2))
 
     def back(i, carry):
-        @pl.when(i == 2)
+        @pl.when(i == 4)
         def _():
             adapter_pieces()
 
-        @pl.when(i == 4)
+        @pl.when(i == 6)
         def _():
             adapter_chip()
-
-        @pl.when(i == 7)
-        def _():
-            adapter_sums()
 
         dx, other = back_place(i)
         p = lax.rem(x + dx, 4) * 2 + jnp.where(other == 1, 1 - zh, zh)
@@ -482,12 +487,28 @@
 
     lax.fori_loop(0, 8, back, 0)
 
+    def over_x(e, s):
+        sum_ = stage[7 - e, s].astype(F32)
+        for d in range(2):
+            x_part_copy(d, e, s).wait_recv()
+            sum_ = sum_ + x_part[d, e, s].astype(F32)
+        return sum_
+
+    def over_x_to(a):
+        z_sum[a] = over_x(0 if a == 0 else 1, z_coords[a][0]).astype(BF16)
+        z_part_copy(a).start()
+
+    over_x_to(2)
+    over_x_to(1)
     total = stage[3, zl].astype(F32)
     for a in range(3):
         z_first_copy(a).wait_recv()
         total = total + z_first[a].astype(F32)
     z_first_sum[...] = total.astype(BF16)
     far_copy().start()
+
+    adapter_sums()
+    over_x_to(0)
 
     def drain(j, carry):
         for n in range(14):
@@ -506,17 +527,6 @@
             ef_out(d, m).wait_send()
     len_copy(zl).wait_send()
 
-    def over_x(e, s):
-        sum_ = stage[7 - e, s].astype(F32)
-        for d in range(2):
-            x_part_copy(d, e, s).wait_recv()
-            sum_ = sum_ + x_part[d, e, s].astype(F32)
-        return sum_
-
-    for a in (2, 1, 0):
-        z_sum[a] = over_x(0 if a == 0 else 1, z_coords[a][0]).astype(BF16)
-        z_part_copy(a).start()
-
     for o in range(1, 8):
         spread_copy(o, chip(8 - o)).wait_recv()
     return_copy(c).start()
@@ -524,19 +534,28 @@
     return_copy(1 - c).wait_recv()
     for r in range(16):
         first_up = r // 2 % 2 * half + (r // 4 * 2 + r % 2) * FEATURES
-        kd_ref[:, r * 256 : r * 256 + 256] = A_all[r // 2, r % 2, 0:16, 0:256]
-        vd_ref[:, r * 256 : r * 256 + 256] = A_all[r // 2, r % 2, 16:32, 0:256]
-        ku_ref[:, pl.ds(first_up, FEATURES)] = A_all[r // 2, r % 2, 0:16, 256:384]
-        vu_ref[:, pl.ds(first_up, FEATURES)] = A_all[r // 2, r % 2, 16:32, 256:384]
+        for t in range(2):
+            rows = slice(16 * t, 16 * t + 16)
+            down_out[t, :, r * 256 : r * 256 + 256] = A_all[r // 2, r % 2, rows, 0:256].astype(F32)
+            up_out[t, :, pl.ds(first_up, FEATURES)] = A_all[r // 2, r % 2, rows, 256:384].astype(F32)
+    leave = [
+        pltpu.make_async_copy(source.at[t], ref, out_sem.at[n])
+        for n, (source, t, ref) in enumerate(
+            ((down_out, 0, kd_ref), (up_out, 0, ku_ref), (down_out, 1, vd_ref), (up_out, 1, vu_ref))
+        )
+    ]
+    for copy in leave:
+        copy.start()
 
     total = over_x(0, zl)
-    far_copy().wait_recv()
-    total = total + x_far[...].astype(F32)
     for a in (2, 1, 0):
         z_part_copy(a).wait_recv()
         total = total + z_part[a].astype(F32)
-    out_ref[...] = total.astype(BF16)
-
+    far_copy().wait_recv()
+    out_ref[...] = (total + x_far[...].astype(F32)).astype(BF16)
+
+    for copy in leave:
+        copy.wait()
     for a in range(3):
         z_first_copy(a).wait_send()
         z_part_copy(a).wait_send()
@@ -553,11 +572,15 @@
 
 
 def settle(*refs):
-    sem = refs[-1]
-    copies = [pltpu.make_async_copy(refs[i], refs[5 + i], sem.at[i]) for i in range(5)]
-    for copy in copies:
+    sources, targets, held, sem = refs[:5], refs[5:10], refs[10:15], refs[15]
+    into = [pltpu.make_async_copy(sources[i], held[i], sem.at[0, i]) for i in range(5)]
+    out = [pltpu.make_async_copy(held[i], targets[i], sem.at[1, i]) for i in range(5)]
+    for copy in into:
         copy.start()
-    for copy in copies:
+    for i in range(5):
+        into[i].wait()
+        out[i].start()
+    for copy in out:
         copy.wait()
 
 
@@ -583,7 +606,7 @@
             jax.ShapeDtypeStruct((16, inner), F32),
         ),
         in_specs=[hbm, hbm, hbm, pl.BlockSpec(memory_space=pltpu.SMEM)] + [hbm] * 6,
-        out_specs=(vmem,) * 5,
+        out_specs=(vmem,) + (hbm,) * 4,
         scratch_shapes=[
             pltpu.VMEM((chunks, 4, 2, 2, BLOCK, PACK), BF16),
             pltpu.VMEM((2, BLOCK, width), BF16),
@@ -607,8 +630,11 @@
             pltpu.VMEM((8, 32, 384), BF16),
             pltpu.VMEM((8, 32, 384), BF16),
             pltpu.VMEM((8, 32, 384), BF16),
-            pltpu.VMEM((8, 2, 32, 384), F32),
+            pltpu.VMEM((8, 2, 32, 384), BF16),
+            pltpu.VMEM((2, 16, width), F32),
+            pltpu.VMEM((2, 16, inner), F32),
             dma((5,)),
+            dma((4,)),
             dma((chunks, 2)),
             dma((chunks, 2)),
             dma((chunks, 14)),
@@ -647,9 +673,9 @@
     out, kd_grad, ku_grad, vd_grad, vu_grad = pl.pallas_call(
         settle,
         out_shape=tuple(jax.ShapeDtypeStruct(r.shape, r.dtype) for r in results),
-        in_specs=[vmem] * 5,
+        in_specs=[hbm] * 5,
         out_specs=(hbm,) * 5,
-        scratch_shapes=[dma((5,))],
+        scratch_shapes=[pltpu.VMEM(r.shape, r.dtype) for r in results] + [dma((2, 5))],
         name="results",
     )(*results)
     return out, kd_grad.T[None], ku_grad[None], vd_grad.T[None], vu_grad[None]

time: 133 us -> 123 us (0.925)
  Pallas kernels: 132 us -> 121 us
    pallas_call x1, Pallas kernels: 130 us -> 119 us  [per_device(): pl.pallas_call(functools.partial(kernel, chunks), out_shape=(jax.ShapeDty...]
where the time goes in v5:
time: 123 us
  Pallas kernels  121 us (98%)
  between operations  1.29 us (1%)
    pallas_call x1, Pallas kernels, per_device(): pl.pallas_call(functools.partial(kernel, chunks), out_shape=(jax.ShapeDty...  119 us

profile of v5, /device:TPU:1, one launch (start us, length us, event | category | flops | bytes accessed | tf_op | source)
XLA Modules:
  0.0 122.5 jit_solution(6040702946010563744)
XLA Ops:
  1.3 119.2 %adapter_backward.1 = (bf16[256,512]{1,0:T(8,128)(2,1)}, f32[16,4096]{1,0:T(8,128)}, f32[16,2048]{1,0:T(8,128)}, f32[16,4096]{1,0:T(8,128)}, f32[16,2048]{1,0:T(8,128)}) custom-call(bf16[256,512]{1,0:T(8,128)(2,1)} %enc_hbm.1, bf16[1,384,2048]{2,1,0:T(8,128)(2,1)} %q_hbm.1, bf16[1,384,2048]{2,1,0:T(8,128)(2,1)} %g_hbm.1, s32[1]{0:T(128)S(6)} %copy.15.len_ref, ...), custom_call_target="tpu_custom_call" | custom-call | tf_op jit(solution)/shard_map/adapter_backward/pallas_call | solution.py:599
  120.5 2.0 %results.1 = (bf16[256,512]{1,0:T(8,128)(2,1)}, f32[16,4096]{1,0:T(8,128)}, f32[16,2048]{1,0:T(8,128)}, f32[16,4096]{1,0:T(8,128)}, f32[16,2048]{1,0:T(8,128)}) custom-call(bf16[256,512]{1,0:T(8,128)(2,1)} %get-tuple-element.15.refs_0_, f32[16,4096]{1,0:T(8,128)} %get-tuple-element.16.refs_1_, f32[16,2048]{1,0:T(8,128)} %get-tuple-element.17.refs_2_, ...), custom_call_target="tpu_custom_call" | custom-call | tf_op jit(solution)/shard_map/results/pallas_call | solution.py:673

commit v6 on v5

--- a/solution.py
+++ b/solution.py
@@ -271,7 +271,6 @@
         both = dot_nt(states, down[...])
         low[...] = both.astype(BF16)
         low_t[...] = both.T.astype(BF16)
-        lowg[...] = jnp.zeros(lowg.shape, F32)
         up_pack[...] = jnp.zeros(up_pack.shape, BF16)
         for j in range(chunks):
             for t in range(2):
@@ -317,15 +316,6 @@
             return carry
 
         lax.fori_loop(0, 2, sequence, 0)
-        grad = dkv[:, here_columns]
-        lowg[...] += dot_nt(grad, up_pack[j])
-        up_grad = adapter_scale * dot(low_t[...], grad)
-        r = (j // 2) * 2 + zl
-        r_core = lax.rem(j, 2)
-        for t in range(2):
-            A[r, r_core, pl.ds(16 * t, 16), 256:384] = up_grad[
-                16 * t : 16 * t + 16, FEATURES * t : FEATURES * t + FEATURES
-            ].astype(BF16)
 
     def within(j, fn):
         @pl.when(jnp.logical_and(j >= 0, j < chunks))
@@ -385,6 +375,7 @@
 
     lax.fori_loop(0, 2 * (chunks + 3), half_slot, 0)
 
+    lowg[...] = dot_nt(dkv[...], jnp.concatenate([up_pack[j] for j in range(chunks)], axis=1))
     low[...] = (adapter_scale * lowg[...]).astype(BF16)
 
     def core_copy():
@@ -409,6 +400,13 @@
             return carry
 
         lax.fori_loop(0, 8, down_grad, 0, unroll=2)
+        for j in range(chunks):
+            up_grad = adapter_scale * dot(low_t[...], dkv[:, j * PACK : j * PACK + PACK])
+            for t in range(2):
+                A[(j // 2) * 2 + zl, j % 2, 16 * t : 16 * t + 16, 256:384] = up_grad[
+                    16 * t : 16 * t + 16, FEATURES * t : FEATURES * t + FEATURES
+                ].astype(BF16)
+
         core_copy().start()
 
     def adapter_chip():

time: 123 us -> 124 us (level)
  no operation moved by 1% of the time
where the time goes in v6:
time: 124 us; the launch traced here: 123 us
  Pallas kernels  121 us (98%)
  between operations  1.29 us (1%)
    pallas_call x1, Pallas kernels, per_device(): pl.pallas_call(functools.partial(kernel, chunks), out_shape=(jax.ShapeDty...  119 us

profile of v6, /device:TPU:1, one launch (start us, length us, event | category | flops | bytes accessed | tf_op | source)
XLA Modules:
  0.0 122.8 jit_solution(1324492953740269556)
XLA Ops:
  1.3 119.5 %adapter_backward.1 = (bf16[256,512]{1,0:T(8,128)(2,1)}, f32[16,4096]{1,0:T(8,128)}, f32[16,2048]{1,0:T(8,128)}, f32[16,4096]{1,0:T(8,128)}, f32[16,2048]{1,0:T(8,128)}) custom-call(bf16[256,512]{1,0:T(8,128)(2,1)} %enc_hbm.1, bf16[1,384,2048]{2,1,0:T(8,128)(2,1)} %q_hbm.1, bf16[1,384,2048]{2,1,0:T(8,128)(2,1)} %g_hbm.1, s32[1]{0:T(128)S(6)} %copy.15.len_ref, ...), custom_call_target="tpu_custom_call" | custom-call | tf_op jit(solution)/shard_map/adapter_backward/pallas_call | solution.py:597
  120.8 2.0 %results.1 = (bf16[256,512]{1,0:T(8,128)(2,1)}, f32[16,4096]{1,0:T(8,128)}, f32[16,2048]{1,0:T(8,128)}, f32[16,4096]{1,0:T(8,128)}, f32[16,2048]{1,0:T(8,128)}) custom-call(bf16[256,512]{1,0:T(8,128)(2,1)} %get-tuple-element.15.refs_0_, f32[16,4096]{1,0:T(8,128)} %get-tuple-element.16.refs_1_, f32[16,2048]{1,0:T(8,128)} %get-tuple-element.17.refs_2_, ...), custom_call_target="tpu_custom_call" | custom-call | tf_op jit(solution)/shard_map/results/pallas_call | solution.py:671
